TPU v7x, 128 devices: a whole 4x4x4 slice. The times are simulated.
128 devices in a mesh: cube: 2 (over core), row: 4 (over x), col: 16 (over z, y).
Axes of the slice: x: 4, y: 4, z: 4, core: 2. Of those that a mesh axis runs over, the one named last changes fastest.
Arguments:
- front_init: float32 [2, 6144, 6144], P('cube', 'row', 'col'), may hold values from -4 to 30, as said below
- contribution: bfloat16 [2, 2048, 2048], P('cube', 'row', 'col'), may hold values from -1 to 2, as said below
- maps: int32 [2, 16], P('cube'), may hold values from 0 to 47, as said below
Outputs:
- factored: float32 [2, 6144, 6144], P('cube', 'row', 'col')
Inputs may be any that keep to these rules, and one draw needn't show every extreme that they name: Each row of maps increases strictly, starts at 0, ends at 47, and its fourth entry lies between 33 and 35. front_init is symmetric; front_init plus any extend-added contribution block is positive definite. contribution is symmetric.
All inputs are finite; a program needn't handle non-finite values.
Results may differ from a plain program's by a relative error of at most 0.0014.
Values may be sent and summed in bfloat16 or wider, within the bound.
No kernel may reach another device: no remote copies, remote signals or barrier semaphores. Data moves between devices by JAX's collectives and lax.ppermute only.
A program may use at most 128 MiB of HBM per device.

v0:
```python
import jax
import jax.numpy as jnp
from jax import lax
from jax.sharding import PartitionSpec as P

BLK = 128
PANEL = 384
PANELS = 4


def swapped(value, axis, apart):
    return lax.ppermute(value, axis, [(i, i ^ 1 << apart) for i in range(lax.axis_size(axis))])


def from_root(value, axis, source):
    kept = jnp.where(lax.axis_index(axis) == source, value, 0).astype(value.dtype)
    return lax.psum(kept, axis)


def child_index(index_map, positions):
    front_blocks = positions // BLK
    hits = front_blocks[:, None] == index_map[None, :]
    found = jnp.any(hits, axis=1)
    counter = jnp.arange(index_map.shape[0], dtype=jnp.int32)
    which = jnp.sum(jnp.where(hits, counter[None, :], 0), axis=1)
    return (found, which * BLK + positions % BLK)


def select_rows(whole, found, source):
    taken = jnp.take(whole, jnp.clip(source, 0, whole.shape[0] - 1), axis=0)
    return jnp.where(found[:, None], taken, jnp.zeros_like(taken))


def select_cols(whole, found, source):
    taken = jnp.take(whole, jnp.clip(source, 0, whole.shape[1] - 1), axis=1)
    return jnp.where(found[None, :], taken, jnp.zeros_like(taken))


def build_panel(panel_cols, factor, global_rows, first_col, end_col):
    lower_part = lax.linalg.triangular_solve(
        factor, panel_cols, left_side=False, lower=True, transpose_a=True
    )
    inside = (global_rows >= first_col) & (global_rows < end_col)
    beneath = global_rows >= end_col
    picked = jnp.take(factor, jnp.clip(global_rows - first_col, 0, factor.shape[0] - 1), axis=0)
    return jnp.where(beneath[:, None], lower_part, jnp.where(inside[:, None], picked, 0.0))


def per_device(front_init, contribution, maps):
    rows_local = front_init.shape[1]
    cols_local = front_init.shape[2]
    n_col = lax.axis_size("col")
    row_id = lax.axis_index("row")
    col_id = lax.axis_index("col")
    global_rows = row_id * rows_local + jnp.arange(rows_local, dtype=jnp.int32)
    global_cols = col_id * cols_local + jnp.arange(cols_local, dtype=jnp.int32)
    received = swapped(contribution[0], "cube", 0)
    found_rows, source_rows = child_index(maps[0], global_rows)
    found_cols, source_cols = child_index(maps[0], global_cols)
    all_rows = lax.all_gather(received, "row", axis=0, tiled=True)
    placed_rows = select_rows(all_rows, found_rows, source_rows)
    all_cols = lax.all_gather(placed_rows, "col", axis=1, tiled=True)
    spread = select_cols(all_cols, found_cols, source_cols)
    frontal = front_init[0] + spread.astype(jnp.float32)
    for panel_index in range(PANELS):
        first_col = panel_index * PANEL
        end_col = first_col + PANEL
        row_owner = first_col // rows_local
        col_owner = first_col // cols_local
        row_offset = first_col - row_owner * rows_local
        col_offset = first_col - col_owner * cols_local
        local_diagonal = frontal[row_offset : row_offset + PANEL, col_offset : col_offset + PANEL]
        diagonal = from_root(local_diagonal, ("row", "col"), row_owner * n_col + col_owner)
        factor = jnp.linalg.cholesky(diagonal)
        local_panel = frontal
        arrived = from_root(local_panel.astype(jnp.bfloat16), "col", col_owner).astype(
            local_panel.dtype
        )
        panel_full = build_panel(arrived, factor, global_rows, first_col, end_col)
        rounded = panel_full.astype(jnp.bfloat16)
        source_row = col_id * cols_local // rows_local
        across = from_root(rounded, "row", source_row)
        column_panel = lax.dynamic_slice_in_dim(
            across, col_id * cols_local - source_row * rows_local, cols_local, 0
        )
        update = lax.dot_general(
            rounded, column_panel, (((1,), (1,)), ((), ())), preferred_element_type=jnp.float32
        )
        trailing = (global_rows >= end_col)[:, None] & (global_cols >= end_col)[None, :]
        frontal = frontal - jnp.where(trailing, update, 0.0)
        previous = frontal
        frontal = frontal.at[:, col_offset : col_offset + PANEL].set(
            jnp.where(col_id == col_owner, panel_full, previous)
        )
    return frontal[None]


def solution(mesh):
    return jax.shard_map(
        per_device,
        mesh=mesh,
        in_specs=(P("cube", "row", "col"), P("cube", "row", "col"), P("cube", None)),
        out_specs=P("cube", "row", "col"),
        check_vma=False,
    )
```

profile of v0, /device:TPU:46, one launch (start us, length us, event | category | flops | bytes accessed | tf_op | source)
XLA Modules:
  0.0 1303.8 jit_solution(1434675799305803821)
XLA Ops:
  8.2 13.4 %all_gather.6 = bf16[2048,128]{1,0:T(8,128)(2,1)S(1)} all-gather(bf16[512,128]{1,0:T(8,128)(2,1)S(1)} %collective-permute-done), channel_id=1, replica_groups=mesh['cube'=2,'row'=4,'col'=16] {'row'}, dimensions={0}, use_global_device_ids=true | all-gather | bytes 655360 | tf_op jit(solution)/shard_map/all_gather | solution.py:60
  21.6 3.2 gather_fusion
  24.8 1.7 select_select_fusion.4
  26.6 2.0 copy.34
  29.0 65.7 %all-gather.2.cloned.1.call-done = bf16[1536,2048]{1,0:T(8,128)(2,1)} async-done(((bf16[1536,128]{1,0:T(8,128)(2,1)}), bf16[1536,2048]{1,0:T(8,128)(2,1)}) %all-gather.2.cloned.1.call-update) | async-done | bytes 6291472 | tf_op jit(solution)/shard_map/all_gather | solution.py:62
  94.6 8.6 copy.35
  103.3 7.3 gather_fusion.1
  115.3 124.4 %all-reduce.14.cloned.1.call-done = f32[384,384]{0,1:T(8,128)} async-done(((f32[384,384]{0,1:T(8,128)}), f32[384,384]{0,1:T(8,128)}) %all-reduce.14.cloned.1.call-update) | async-done | bytes 589840 | tf_op jit(solution)/shard_map/psum | solution.py:17
  242.1 11.7 cholesky.338
  253.9 9.8 custom-call.26
  264.3 11.7 cholesky.357
  276.1 10.2 custom-call.27
  286.8 11.7 cholesky.376
  301.9 6.2 while.16
  308.1 30.1 %custom-call.28 = f32[3,128,128]{1,2,0:T(8,128)} custom-call(f32[3,128,128]{2,1,0:T(8,128)S(1)} %get-tuple-element.114), custom_call_target="InvertDiagBlocksLowerTriangular" | custom-call | tf_op jit(solution)/shard_map/triangular_solve/custom-call.2 | solution.py:40
  338.3 3.7 gather_fusion.2
  342.0 2.0 copy.39
  348.2 2.2 convolution_subtract_fusion.3
  350.5 1.7 fusion.81
  354.8 46.9 %all-reduce.18.cloned.1.call-done = bf16[1536,384]{0,1:T(8,128)(2,1)} async-done(((bf16[1536,384]{0,1:T(8,128)(2,1)}), bf16[1536,384]{0,1:T(8,128)(2,1)}) %all-reduce.18.cloned.1.call-update) | async-done | bytes 1179664 | tf_op jit(solution)/shard_map/psum | solution.py:17
  401.7 5.0 convert_select_fusion.2
  410.0 125.0 %all-reduce.20.cloned.1.call-done = f32[384,384]{0,1:T(8,128)} async-done(((f32[384,384]{0,1:T(8,128)}), f32[384,384]{0,1:T(8,128)}) %all-reduce.20.cloned.1.call-update) | async-done | bytes 589840 | tf_op jit(solution)/shard_map/psum | solution.py:17
  537.4 11.7 cholesky.391
  549.2 9.8 custom-call.29
  559.6 11.7 cholesky.410
  572.8 10.2 custom-call.30
  583.4 11.7 cholesky.429
  597.8 6.2 while.17
  604.0 30.1 %custom-call.31 = f32[3,128,128]{1,2,0:T(8,128)} custom-call(f32[3,128,128]{2,1,0:T(8,128)S(1)} %get-tuple-element.115), custom_call_target="InvertDiagBlocksLowerTriangular" | custom-call | tf_op jit(solution)/shard_map/triangular_solve/custom-call.2 | solution.py:40
  634.2 3.7 gather_fusion.3
  637.9 2.0 copy.44
  644.1 2.2 convolution_subtract_fusion.2
  646.4 1.7 fusion.76
  650.7 46.9 %all-reduce.24.cloned.1.call-done = bf16[1536,384]{0,1:T(8,128)(2,1)} async-done(((bf16[1536,384]{0,1:T(8,128)(2,1)}), bf16[1536,384]{0,1:T(8,128)(2,1)}) %all-reduce.24.cloned.1.call-update) | async-done | bytes 1179664 | tf_op jit(solution)/shard_map/psum | solution.py:17
  697.6 5.0 convert_select_fusion.1
  705.9 125.0 %all-reduce.26.cloned.1.call-done = f32[384,384]{0,1:T(8,128)} async-done(((f32[384,384]{0,1:T(8,128)}), f32[384,384]{0,1:T(8,128)}) %all-reduce.26.cloned.1.call-update) | async-done | bytes 589840 | tf_op jit(solution)/shard_map/psum | solution.py:17
  833.3 11.7 cholesky.444
  845.1 9.8 custom-call.32
  855.5 11.7 cholesky.463
  868.7 10.2 custom-call.33
  879.3 11.7 cholesky.482
  893.7 6.2 while.18
  899.9 30.1 %custom-call.34 = f32[3,128,128]{1,2,0:T(8,128)} custom-call(f32[3,128,128]{2,1,0:T(8,128)S(1)} %get-tuple-element.116), custom_call_target="InvertDiagBlocksLowerTriangular" | custom-call | tf_op jit(solution)/shard_map/triangular_solve/custom-call.2 | solution.py:40
  930.1 3.7 gather_fusion.4
  933.8 2.0 copy.49
  940.0 2.2 convolution_subtract_fusion.1
  942.3 1.7 fusion.71
  946.6 46.9 %all-reduce.30.cloned.1.call-done = bf16[1536,384]{0,1:T(8,128)(2,1)} async-done(((bf16[1536,384]{0,1:T(8,128)(2,1)}), bf16[1536,384]{0,1:T(8,128)(2,1)}) %all-reduce.30.cloned.1.call-update) | async-done | bytes 1179664 | tf_op jit(solution)/shard_map/psum | solution.py:17
  993.5 5.0 convert_select_fusion
  1001.8 124.9 %all-reduce.32.cloned.1.call-done = f32[384,384]{0,1:T(8,128)} async-done(((f32[384,384]{0,1:T(8,128)}), f32[384,384]{0,1:T(8,128)}) %all-reduce.32.cloned.1.call-update) | async-done | bytes 589840 | tf_op jit(solution)/shard_map/psum | solution.py:17
  1129.1 11.7 cholesky.497
  1140.9 9.8 custom-call.35
  1151.3 11.7 cholesky.516
  1164.4 10.0 custom-call.36
  1174.9 11.7 cholesky.535
  1189.3 5.8 while.19
  1195.1 30.1 %custom-call.37 = f32[3,128,128]{1,2,0:T(8,128)} custom-call(f32[3,128,128]{2,1,0:T(8,128)S(1)} %get-tuple-element.117), custom_call_target="InvertDiagBlocksLowerTriangular" | custom-call | tf_op jit(solution)/shard_map/triangular_solve/custom-call.2 | solution.py:40
  1225.2 3.7 gather_fusion.5
  1229.0 2.0 copy.54
  1235.2 2.2 convolution_subtract_fusion
  1237.5 1.7 fusion.66
  1241.7 47.0 %all-reduce.36.cloned.1.call-done = bf16[1536,384]{0,1:T(8,128)(2,1)} async-done(((bf16[1536,384]{0,1:T(8,128)(2,1)}), bf16[1536,384]{0,1:T(8,128)(2,1)}) %all-reduce.36.cloned.1.call-update) | async-done | bytes 1179664 | tf_op jit(solution)/shard_map/psum | solution.py:17
  1288.7 5.3 fusion.8
  1294.0 3.0 copy.56
  (262 shorter events, 89.5 us)
Async XLA Ops:
  6.5 88.1 %all-gather.2.cloned.1.call-start = ((), (), s32[]{:S(2)}) async-start(), calls=%async_computation | async-start | bytes 6684672 | tf_op jit(solution)/shard_map/all_gather | solution.py:62
  6.5 1.6 collective-permute-start
  26.6 213.1 %all-reduce.14.cloned.1.call-start = ((), (), s32[]{:S(2)}) async-start(), calls=%async_computation.1 | async-start | bytes 1179648 | tf_op jit(solution)/shard_map/psum | solution.py:17
  26.6 2.1 copy-start.32
  112.0 1.4 copy-start.8
  114.3 229.7 %all-reduce.16.cloned.1.call-start = ((), (), s32[]{:S(2)}) async-start(), calls=%async_computation.2 | async-start | bytes 2359296 | tf_op jit(solution)/shard_map/psum | solution.py:17
  115.1 286.6 %all-reduce.18.cloned.1.call-start = ((), (), s32[]{:S(2)}) async-start(), calls=%async_computation.3 | async-start | bytes 2359296 | tf_op jit(solution)/shard_map/psum | solution.py:17
  308.1 38.3 %copy-start.14 = (f32[384,384]{1,0:T(8,128)}, f32[384,384]{1,0:T(8,128)S(1)}, u32[]{:S(2)}) copy-start(f32[384,384]{1,0:T(8,128)S(1)} %get-tuple-element.433) | copy-start | bytes 1769476
  344.0 1.6 copy-start.17
  348.2 4.0 copy-start.4
  348.2 4.9 copy-start
  348.2 4.9 copy-start.24
  348.2 4.9 copy-start.25
  352.2 0.9 copy-start.9
  354.7 180.3 %all-reduce.20.cloned.1.call-start = ((), (), s32[]{:S(2)}) async-start(), calls=%async_computation.4 | async-start | bytes 1179648 | tf_op jit(solution)/shard_map/psum | solution.py:17
  406.7 1.4 copy-start.22
  409.0 230.9 %all-reduce.22.cloned.1.call-start = ((), (), s32[]{:S(2)}) async-start(), calls=%async_computation.5 | async-start | bytes 2359296 | tf_op jit(solution)/shard_map/psum | solution.py:17
  409.8 287.9 %all-reduce.24.cloned.1.call-start = ((), (), s32[]{:S(2)}) async-start(), calls=%async_computation.6 | async-start | bytes 2359296 | tf_op jit(solution)/shard_map/psum | solution.py:17
  604.0 38.3 %copy-start.15 = (f32[384,384]{1,0:T(8,128)}, f32[384,384]{1,0:T(8,128)S(1)}, u32[]{:S(2)}) copy-start(f32[384,384]{1,0:T(8,128)S(1)} %get-tuple-element.434) | copy-start | bytes 1769476
  639.9 1.6 copy-start.18
  644.1 4.0 copy-start.6
  644.1 4.9 copy-start.2
  644.1 4.9 copy-start.28
  644.1 4.9 copy-start.29
  648.1 0.9 copy-start.11
  650.6 180.3 %all-reduce.26.cloned.1.call-start = ((), (), s32[]{:S(2)}) async-start(), calls=%async_computation.7 | async-start | bytes 1179648 | tf_op jit(solution)/shard_map/psum | solution.py:17
  702.7 1.4 copy-start.21
  705.0 230.8 %all-reduce.28.cloned.1.call-start = ((), (), s32[]{:S(2)}) async-start(), calls=%async_computation.8 | async-start | bytes 2359296 | tf_op jit(solution)/shard_map/psum | solution.py:17
  705.7 287.8 %all-reduce.30.cloned.1.call-start = ((), (), s32[]{:S(2)}) async-start(), calls=%async_computation.9 | async-start | bytes 2359296 | tf_op jit(solution)/shard_map/psum | solution.py:17
  899.9 38.3 %copy-start.16 = (f32[384,384]{1,0:T(8,128)}, f32[384,384]{1,0:T(8,128)S(1)}, u32[]{:S(2)}) copy-start(f32[384,384]{1,0:T(8,128)S(1)} %get-tuple-element.435) | copy-start | bytes 1769476
  935.8 1.6 copy-start.19
  940.0 4.0 copy-start.5
  940.0 4.9 copy-start.1
  940.0 4.9 copy-start.26
  940.0 4.9 copy-start.27
  944.0 0.9 copy-start.10
  946.5 180.2 %all-reduce.32.cloned.1.call-start = ((), (), s32[]{:S(2)}) async-start(), calls=%async_computation.10 | async-start | bytes 1179648 | tf_op jit(solution)/shard_map/psum | solution.py:17
  998.6 1.4 copy-start.23
  1000.9 230.1 %all-reduce.34.cloned.1.call-start = ((), (), s32[]{:S(2)}) async-start(), calls=%async_computation.11 | async-start | bytes 2359296 | tf_op jit(solution)/shard_map/psum | solution.py:17
  1001.6 287.1 %all-reduce.36.cloned.1.call-start = ((), (), s32[]{:S(2)}) async-start(), calls=%async_computation.12 | async-start | bytes 2359296 | tf_op jit(solution)/shard_map/psum | solution.py:17
  1195.1 38.3 %copy-start.13 = (f32[384,384]{1,0:T(8,128)}, f32[384,384]{1,0:T(8,128)S(1)}, u32[]{:S(2)}) copy-start(f32[384,384]{1,0:T(8,128)S(1)} %get-tuple-element.432) | copy-start | bytes 1769476
  1231.0 1.6 copy-start.20
  1235.2 4.0 copy-start.7
  1235.2 4.9 copy-start.3
  1235.2 4.9 copy-start.30
  1235.2 4.9 copy-start.31
  1239.2 0.9 copy-start.12
Sparse Core Ops, SparseCore 0:
  26.7 67.9 all-gather.1
  114.4 125.2 all-reduce.13
  243.4 86.7 all-reduce.15
  354.8 46.8 all-reduce.17
  409.1 125.8 all-reduce.19
  538.1 87.0 all-reduce.21
  650.8 46.8 all-reduce.23
  705.1 125.7 all-reduce.25
  834.6 86.7 all-reduce.27
  946.6 46.8 all-reduce.29
  1001.0 125.6 all-reduce.31
  1129.9 86.9 all-reduce.33
  1241.8 46.8 all-reduce.35
where the time goes:
time: 1310 us; the launch traced here: 1300 us
  waiting for transfers between devices  753 us (57%)
  other arithmetic  377 us (29%)
  local copies, waits for them, and re-layouts  86.1 us (7%)
  matrix products  50.4 us (4%)
  between operations  22.2 us (2%)
  blocking collectives  13.4 us (1%)
    psum x12, waiting for transfers between devices, from_root(): return lax.psum(kept, axis)  687 us
    another operation x43, other arithmetic, per_device(): factor = jnp.linalg.cholesky(diagonal)  228 us
    another operation x9, other arithmetic, build_panel(): lax.linalg.triangular_solve(factor, panel_cols, left_side=False, lower=Tr...  121 us
    all_gather x1, waiting for transfers between devices, per_device(): all_cols = lax.all_gather(placed_rows, 'col', axis=1, tiled=True)  65.7 us
  transfers between devices with their start and end apart: 14, of which 9 were waited for; matrix products, arithmetic and copies ran while one was open for 32% of the time, Pallas kernels for 0%

commit v1 on v0

v1 whole, which is shorter than its diff:
```python
import functools

import jax
import jax.numpy as jnp
from jax import lax
from jax.experimental import pallas as pl
from jax.experimental.pallas import tpu as pltpu
from jax.sharding import PartitionSpec as P

BLK = 128
PANEL = 384
PANELS = 4
N_ROW = 4
N_COL = 16
PIECE = PANEL // N_ROW
LEAD = PANEL * PANELS
F32 = jnp.float32
BF16 = jnp.bfloat16

SOURCES = {11: [3, 4, 5], 12: [4, 5, 6, 7, 8], 13: [7, 8, 9, 10, 11], 14: [10, 11, 12, 13, 14], 15: [13, 14, 15]}
THICK = 5


def dot(a, b, ca, cb):
    return lax.dot_general(a, b, (((ca,), (cb,)), ((), ())), preferred_element_type=F32)


def split(x):
    high = x.astype(BF16)
    return high, (x - high.astype(F32)).astype(BF16)


def dot3(a, b, ca, cb):
    ah, al = split(a)
    bh, bl = split(b)
    return dot(jnp.concatenate([ah, ah, al], ca), jnp.concatenate([bh, bl, bh], cb), ca, cb)


def over_rows(x, i):
    return jnp.broadcast_to(x[i : i + 1, :], x.shape)


def over_lanes(x, j):
    return jnp.broadcast_to(x[:, j : j + 1], x.shape)


def factor_block(tiles, group=4):
    sub = lax.broadcasted_iota(jnp.int32, (8, BLK), 0)
    lane = lax.broadcasted_iota(jnp.int32, (8, BLK), 1)
    v = list(tiles)
    inv, upper, scale = [None] * 16, [None] * 16, [None] * 16
    for g in range(0, 16, group):
        for t in range(g, g + group):
            qs = range(t, g + group)
            c = {(q, j): over_lanes(v[q], 8 * t + j) for q in qs for j in range(8)}
            block = (lane >= 8 * t) & (lane < 8 * t + 8)
            sc = jnp.zeros((8, BLK), F32)
            w = {q: jnp.where(block, 0.0, v[q]) for q in qs}
            w[t] = jnp.where(lane - 8 * t == sub, 1.0, w[t])
            u = v[t]
            for i in range(8):
                pivot = over_rows(c[t, i], i)
                r = 1.0 / pivot
                sc = jnp.where(sub == i, lax.rsqrt(pivot), sc)
                m = {q: c[q, i] * r for q in qs}
                m[t] = jnp.where(sub > i, m[t], 0.0)
                for j in range(i + 1, 8):
                    row = over_rows(c[t, j], i)
                    for q in qs:
                        c[q, j] = c[q, j] - m[q] * row
                row = over_rows(w[t], i)
                for q in qs:
                    if q != t or i < 7:
                        w[q] = w[q] - m[q] * row
                if i < 7:
                    u = u - m[t] * over_rows(u, i)
            inv[t], scale[t], upper[t] = w[t], sc, u
            for q in range(t + 1, g + group):
                v[q] = w[q]
        if g + group < 16:
            sg = jnp.concatenate(scale[g : g + group], 0)
            ug = jnp.concatenate(upper[g : g + group], 0) * sg
            done = [
                jnp.where((lane >= 8 * t + 8) & (lane < 8 * g + 8 * group), 0.0, inv[t]) for t in range(g, g + group)
            ]
            wg = jnp.concatenate(done, 0) * sg
            update = dot3(ug, wg, 0, 0)
            block = (lane >= 8 * g) & (lane < 8 * g + 8 * group)
            for q in range(g + group, 16):
                v[q] = jnp.where(block, 0.0, v[q]) - update[8 * q : 8 * q + 8, :]
    return [a * s for a, s in zip(inv, scale)], [a * s for a, s in zip(upper, scale)]


def factor_panel(p, li, ud):
    sub = lax.broadcasted_iota(jnp.int32, (8, BLK), 0)
    lane = lax.broadcasted_iota(jnp.int32, (8, BLK), 1)

    def step(j, _):
        at = pl.multiple_of(j * BLK, BLK)
        inv, upper = factor_block([p[pl.ds(at + 8 * q, 8), pl.ds(at, BLK)] for q in range(16)])
        for q in range(16):
            li[8 * q : 8 * q + 8, :] = jnp.where(lane <= sub + 8 * q, inv[q], 0.0)
            ud[pl.ds(at + 8 * q, 8), :] = jnp.where(lane >= sub + 8 * q, upper[q], 0.0)
        row = dot3(li[...], p[pl.ds(at, BLK), :], 1, 0)
        p[pl.ds(at, BLK), :] = row
        p[pl.ds(at, BLK), pl.ds(at, BLK)] = li[...]
        for k in range(1, 3):

            @pl.when(k > j)
            def _():
                rows = slice(k * BLK, k * BLK + BLK)
                p[rows, pl.ds(at, BLK)] = jnp.zeros((BLK, BLK), F32)
                p[rows, :] = p[rows, :] - dot3(row[:, rows], p[pl.ds(at, BLK), :], 0, 0)

        return 0

    lax.fori_loop(0, 3, step, 0)


def panel_kernel(k, base, info, maps, *refs):
    r = list(refs)
    pieces, r = r[:4], r[4:]
    t_pieces, r = r[:4], r[4:]
    ups, r = r[:k], r[k:]
    invs, r = r[: 2 * k], r[2 * k :]
    inv_hi, inv_lo, up_out, low_out, mine_out = r[:5]
    a, t, p, li, ud = r[5:]
    me = info[0]
    col = info[1]
    for s in range(4):
        at = pl.multiple_of(lax.rem(me + 4 - s, 4) * PIECE, PIECE)
        buf = pieces[s]
        for j in range(k):
            a[pl.ds(j * PANEL + at, PIECE), :] = buf[base + (2 + j) * PIECE : base + (3 + j) * PIECE, :].astype(F32)
        a[pl.ds(k * PANEL + at, PIECE), :] = buf[base : base + PIECE, :].astype(F32) + buf[
            base + PIECE : base + 2 * PIECE, :
        ].astype(F32)
        for b in range(3):
            for u in range(3):
                t[pl.ds(at + 32 * u, 32), b * BLK : (b + 1) * BLK] = t_pieces[s][
                    2 * PIECE + 32 * b : 2 * PIECE + 32 * b + 32, u * BLK : (u + 1) * BLK
                ].astype(F32)
    for b in range(3):
        mb = maps[b] - 3 * k
        for i in range(3):
            ma = maps[i]

            @pl.when((mb >= 0) & (mb < 3) & (ma < 3 * (k + 1)))
            def _():
                rows = pl.ds(pl.multiple_of(ma * BLK, BLK), BLK)
                cols = pl.ds(pl.multiple_of(mb * BLK, BLK), BLK)
                a[rows, cols] = a[rows, cols] + t[i * BLK : (i + 1) * BLK, b * BLK : (b + 1) * BLK]

    mine_out[...] = jnp.zeros((PANEL, PANEL), F32)
    cur = []
    for j in range(k):
        z = a[j * PANEL : (j + 1) * PANEL, :]
        for i in range(j):
            z = z - dot(ups[j][i * PANEL : (i + 1) * PANEL, :], cur[i], 0, 0)
        zh, zl = split(z)
        ih, il = invs[2 * j][...], invs[2 * j + 1][...]
        uf = dot(ih, zh, 1, 0) + (dot(ih, zl, 1, 0) + dot(il, zh, 1, 0))

        @pl.when(col == j)
        def _():
            mine_out[...] = uf.T

        ub = uf.astype(BF16)
        up_out[j * PANEL : (j + 1) * PANEL, :] = ub
        cur.append(ub)
    if k == 0:
        up_out[...] = jnp.zeros(up_out.shape, BF16)
    z = a[k * PANEL : (k + 1) * PANEL, :]
    for j in range(k):
        z = z - dot(cur[j], cur[j], 0, 0)
    p[...] = z
    factor_panel(p, li, ud)
    for i in range(3):
        ri = slice(i * BLK, (i + 1) * BLK)
        for j in range(3):
            rj = slice(j * BLK, (j + 1) * BLK)
            if j <= i:
                hi, lo = split(p[ri, rj])
                inv_hi[ri, rj] = hi
                inv_lo[ri, rj] = lo
            else:
                inv_hi[ri, rj] = jnp.zeros((BLK, BLK), BF16)
                inv_lo[ri, rj] = jnp.zeros((BLK, BLK), BF16)
                low_out[ri, rj] = jnp.zeros((BLK, BLK), F32)
                low_out[rj, ri] = p[ri, rj].T
        low_out[ri, ri] = ud[ri, :].T


def panel_call(k, base, info, maps, pieces, t_pieces, ups, invs):
    vm = pl.BlockSpec(memory_space=pltpu.VMEM)
    sm = pl.BlockSpec(memory_space=pltpu.SMEM)
    args = list(pieces) + list(t_pieces) + list(ups) + list(invs)
    sq = (PANEL, PANEL)
    return pl.pallas_call(
        functools.partial(panel_kernel, k, base),
        out_shape=[
            jax.ShapeDtypeStruct(sq, BF16),
            jax.ShapeDtypeStruct(sq, BF16),
            jax.ShapeDtypeStruct((max(k, 1) * PANEL if k else 16, PANEL), BF16),
            jax.ShapeDtypeStruct(sq, F32),
            jax.ShapeDtypeStruct(sq, F32),
        ],
        in_specs=[sm, sm] + [vm] * len(args),
        out_specs=[vm] * 5,
        scratch_shapes=[
            pltpu.VMEM(((k + 1) * PANEL, PANEL), F32),
            pltpu.VMEM(sq, F32),
            pltpu.VMEM(sq, F32),
            pltpu.VMEM((BLK, BLK), F32),
            pltpu.VMEM((PANEL, BLK), F32),
        ],
        compiler_params=pltpu.CompilerParams(vmem_limit_bytes=40 * 2**20),
        cost_estimate=pl.CostEstimate(flops=10**10, bytes_accessed=10**6, transcendentals=0),
        name=f"panel{k}",
    )(info, maps, *args)


def tail_kernel(info, maps, front, a12, wide, *refs):
    r = list(refs)
    thick, r = r[:THICK], r[THICK:]
    t_pieces, r = r[:4], r[4:]
    ups, r = r[:3], r[3:]
    invs, r = r[:4], r[4:]
    lows, r = r[:4], r[4:]
    mines, r = r[:3], r[3:]
    out = r[0]
    x, t, y = r[1:]
    me = info[0]
    col = info[1]
    first = info[2]
    sq = (PANEL, PANEL)

    def blk(i):
        return slice(i * BLK, (i + 1) * BLK)

    def pan(i):
        return slice(i * PANEL, (i + 1) * PANEL)

    @pl.when((me == 0) & (col < PANELS))
    def _():
        for j in range(PANELS):

            @pl.when(col > j)
            def _():
                out[pan(j), :] = jnp.zeros(sq, F32)

            @pl.when(col == j)
            def _():
                out[pan(j), :] = lows[j][...]

            if j:

                @pl.when(col < j)
                def _():
                    out[pan(j), :] = mines[j - 1][...]

    def add(ref, row_block, col_slot, value):
        rows = pl.ds(pl.multiple_of(row_block * BLK, BLK), BLK)
        cols = pl.ds(pl.multiple_of(col_slot * BLK, BLK), BLK)
        ref[rows, cols] = ref[rows, cols] + value

    @pl.when(col >= PANELS)
    def _():
        @pl.when(me == 0)
        def _():
            x[...] = front[...]

        @pl.when(me != 0)
        def _():
            x[...] = a12[...].astype(F32)

        for s in range(4):
            at = pl.multiple_of(lax.rem(me + 4 - s, 4) * PIECE, PIECE)
            for b in range(3):
                for u in range(3):
                    t[pl.ds(at + 32 * u, 32), blk(b)] = t_pieces[s][
                        2 * PIECE + 32 * b : 2 * PIECE + 32 * b + 32, blk(u)
                    ].astype(F32)
        for i in range(3):
            ma = maps[i]
            for b in range(3):
                slot = maps[b] - 3 * col

                @pl.when((ma < 12) & (slot >= 0) & (slot < 3))
                def _():
                    add(x, ma, slot, t[blk(i), blk(b)])

            for j in range(THICK):
                slot = info[8 + j] - 3 * col

                @pl.when((ma < 12) & (slot >= 0) & (slot < 3))
                def _():
                    add(x, ma, slot, thick[j][blk(i), :].astype(F32))

        xs = []
        for j in range(PANELS):
            z = x[pan(j), :]
            for i in range(j):
                z = z - dot(ups[j - 1][pan(i), :], xs[i], 0, 0)
            xs.append(dot(invs[j][...], z.astype(BF16), 1, 0).astype(BF16))

            @pl.when(me == 0)
            def _():
                out[pan(j), :] = z

        for j in range(PANELS):
            x[pan(j), :] = xs[j].astype(F32)

    @pl.when(me > 0)
    def _():
        @pl.when(col >= PANELS)
        def _():
            out[...] = front[...]
            for q in range(12):
                ma = maps[first + q] - 12 * me

                @pl.when((ma >= 0) & (ma < 12))
                def _():
                    for b in range(3):
                        slot = maps[b] - 3 * col

                        @pl.when((slot >= 0) & (slot < 3))
                        def _():
                            piece = wide[(q // 3) * 4 + b, blk(q % 3), PANEL : PANEL + BLK]
                            add(out, ma, slot, piece.astype(F32))

                    for j in range(THICK):
                        slot = info[8 + j] - 3 * col

                        @pl.when((slot >= 0) & (slot < 3))
                        def _():
                            rows = pl.ds(pl.multiple_of((first + q) * BLK, BLK), BLK)
                            add(out, ma, slot, thick[j][rows, :].astype(F32))

        for z in range(4):
            for k in range(PANELS):
                y[k, pan(z), :] = wide[z * 4 + k, :, :PANEL].astype(F32)
        for q in range(12):
            ma = maps[first + q] - 12 * me

            @pl.when((ma >= 0) & (ma < 12))
            def _():
                for b in range(3):
                    mb = maps[b]

                    @pl.when(mb < 12)
                    def _():
                        panel = mb // 3
                        piece = wide[(q // 3) * 4 + b, blk(q % 3), PANEL : PANEL + BLK].astype(F32)
                        rows = pl.ds(pl.multiple_of(ma * BLK, BLK), BLK)
                        cols = pl.ds(pl.multiple_of((mb - panel * 3) * BLK, BLK), BLK)
                        y[panel, rows, cols] = y[panel, rows, cols] + piece

        def rows_step(q, _):
            rows = pl.ds(pl.multiple_of(q * PANEL, PANEL), PANEL)
            ys = []
            for k in range(PANELS):
                z = y[k, rows, :]
                for i in range(k):
                    z = z - dot(ys[i], ups[k - 1][pan(i), :], 1, 0)
                full = dot(z.astype(BF16), invs[k][...], 1, 1)
                ys.append(full.astype(BF16))

                @pl.when(col == k)
                def _():
                    out[rows, :] = full

            @pl.when(col >= PANELS)
            def _():
                acc = out[rows, :]
                for k in range(PANELS):
                    acc = acc - dot(ys[k], x[pan(k), :].astype(BF16), 1, 0)
                out[rows, :] = acc

            return 0

        lax.fori_loop(0, 4, rows_step, 0)


def tail_call(info, maps, front, a12, wide, thick, t_pieces, ups, invs, lows, mines):
    vm = pl.BlockSpec(memory_space=pltpu.VMEM)
    sm = pl.BlockSpec(memory_space=pltpu.SMEM)
    args = [front, a12, wide, *thick, *t_pieces, *ups, *invs, *lows, *mines]
    return pl.pallas_call(
        tail_kernel,
        out_shape=jax.ShapeDtypeStruct((LEAD, PANEL), F32),
        in_specs=[sm, sm] + [vm] * len(args),
        out_specs=vm,
        scratch_shapes=[
            pltpu.VMEM((LEAD, PANEL), F32),
            pltpu.VMEM((PANEL, PANEL), F32),
            pltpu.VMEM((PANELS, LEAD, PANEL), F32),
        ],
        compiler_params=pltpu.CompilerParams(vmem_limit_bytes=58 * 2**20),
        cost_estimate=pl.CostEstimate(flops=7 * 10**9, bytes_accessed=2 * 10**7, transcendentals=0),
        name="tail",
    )(info, maps, *args)


def per_device(front_init, contribution, maps):
    front = front_init[0]
    index_map = maps[0]
    me = lax.axis_index("row")
    col = lax.axis_index("col")
    y = lax.rem(col, 4)
    grid = ("row", "col")

    def flat(r, c):
        return r * N_COL + c

    def x_from0(value, s, cols):
        return lax.ppermute(value, grid, [(flat(0, c), flat(s, c)) for c in cols])

    def z_from0(value, s):
        return lax.ppermute(value, "col", [(b, 4 * s + b) for b in range(4)])

    def x_shift(value, s):
        return lax.ppermute(value, "row", [(i, (i + s) % 4) for i in range(4)])

    def y_shift(value, s):
        return lax.ppermute(value, "col", [(4 * z + b, 4 * z + (b + s) % 4) for z in range(4) for b in range(4)])

    received = lax.ppermute(contribution[0], "cube", [(0, 1), (1, 0)])

    high = front.astype(BF16)
    diag = lax.dynamic_slice_in_dim(front, y * PANEL, PANEL, 0)
    diag_high = diag.astype(BF16)
    diag_low = (diag - diag_high.astype(F32)).astype(BF16)

    def quarter(s):
        rows = slice(s * PIECE, (s + 1) * PIECE)
        child = received[rows, :]
        child = jnp.concatenate([child[:32], child[32:64], child[64:96]], axis=1)
        offs = [high[j * PANEL + s * PIECE : j * PANEL + (s + 1) * PIECE] for j in range(3)]
        return jnp.concatenate([diag_high[rows], diag_low[rows], *offs, child], axis=0)

    mine = jnp.where(me == 0, quarter(0), jnp.zeros((), BF16))
    for s in range(1, 4):
        mine = mine + x_from0(quarter(s), s, range(4))
    at_root = mine
    spread = jnp.where(col < 4, at_root, jnp.zeros((), BF16))
    for s in range(1, 4):
        spread = spread + z_from0(at_root, s)
    around = [spread] + [y_shift(spread, s) for s in range(1, 4)]
    stacked = jnp.stack(around)
    order = [lax.rem(y + 4 - k, 4) for k in range(4)]
    by_panel = [lax.dynamic_index_in_dim(stacked, order[k], 0, keepdims=False) for k in range(4)]
    r0 = jnp.concatenate([by_panel[0][: 2 * PIECE]] + [by_panel[b][5 * PIECE :] for b in range(3)], axis=0)
    r1 = by_panel[1][: 3 * PIECE]
    r23 = jnp.concatenate([by_panel[2][: 4 * PIECE], by_panel[3][: 5 * PIECE]], axis=0)
    g0 = [r0] + [x_shift(r0, s) for s in range(1, 4)]
    g1 = [r1] + [x_shift(r1, s) for s in range(1, 4)]
    g23 = [r23] + [x_shift(r23, s) for s in range(1, 4)]

    parts = [received] + [x_shift(received, s) for s in range(1, 4)]
    parts = jnp.stack(parts)
    column = jnp.concatenate(
        [lax.dynamic_index_in_dim(parts, lax.rem(me + 4 - i, 4), 0, keepdims=False) for i in range(4)], axis=0
    )
    first = jnp.where(me == 3, 4, 0)
    chosen = lax.dynamic_slice_in_dim(column, first * BLK, 12 * BLK, 0)
    thick = []
    for j in range(THICK):
        pairs = [(SOURCES[c][j], c) for c in SOURCES if j < len(SOURCES[c])]
        thick.append(lax.ppermute(column, "col", pairs))

    panel_wide = jnp.concatenate([high, chosen], axis=1)
    wide = jnp.where(col < 4, panel_wide[:PANEL], jnp.zeros((), BF16))
    for s in range(1, 4):
        wide = wide + z_from0(panel_wide[s * PANEL : (s + 1) * PANEL], s)
    wide = lax.all_gather(wide, "col")
    a12 = high
    got = jnp.zeros((), BF16)
    for s in range(1, 4):
        got = got + x_from0(high, s, range(4, N_COL))
    a12 = got

    ids = jnp.full((N_COL, THICK), -1, jnp.int32)
    for c in SOURCES:
        for j, b in enumerate(SOURCES[c]):
            ids = ids.at[c, j].set(b)
    held = jnp.take(ids, col, axis=0)
    targets = jnp.where(held >= 0, jnp.take(index_map, jnp.maximum(held, 0)), -1000)
    info = jnp.concatenate(
        [jnp.stack([me, col, first, 0, 0, 0, 0, 0]).astype(jnp.int32), targets.astype(jnp.int32), jnp.zeros((3,), jnp.int32)]
    )

    ups, invs, lows, mines = [], [], [], []
    flat_invs = []
    for k in range(PANELS):
        pieces = [g0, g1, g23, g23][k]
        base = 4 * PIECE if k == 3 else 0
        ih, il, up, low, mine_out = panel_call(k, base, info, index_map, pieces, g0, ups, flat_invs)
        flat_invs += [ih, il]
        ups.append(up)
        invs.append(ih)
        lows.append(low)
        mines.append(mine_out)
    out = tail_call(info, index_map, front, a12, wide, thick, g0, ups[1:], invs, lows, mines[1:])
    return out[None]


def solution(mesh):
    return jax.shard_map(
        per_device,
        mesh=mesh,
        in_specs=(P("cube", "row", "col"), P("cube", "row", "col"), P("cube", None)),
        out_specs=P("cube", "row", "col"),
        check_vma=False,
    )
```

time: 1310 us -> 286 us (0.22)
  waiting for transfers between devices: 753 us -> 63.6 us
  other arithmetic: 377 us -> 15.4 us
  Pallas kernels: 0 us -> 102 us
  starting transfers between devices: 1.21 us -> 78.1 us
  local copies, waits for them, and re-layouts: 86.1 us -> 9.52 us
  matrix products: 50.4 us -> 0 us
  blocking collectives: 13.4 us -> 0 us
    psum x12 -> x0, waiting for transfers between devices: 687 us -> none  [from_root(): return lax.psum(kept, axis)]
    another operation x52 -> x2, other arithmetic: 349 us -> 0.31 us  [the longest x1 0.24 us: per_device(): stacked = jnp.stack(around)]
    pallas_call x0 -> x5, Pallas kernels: none -> 102 us  [the longest x4 72.4 us: panel_call(): pl.pallas_call(functools.partial(panel_kernel, k, base), out_shape=[jax.S...]
    ppermute x1 -> x33, starting transfers between devices: 0.01 us -> 78.1 us  [the longest x5 44 us: per_device(): thick.append(lax.ppermute(column, 'col', pairs))]
    all_gather x1, waiting for transfers between devices: 65.7 us -> 0.01 us  [per_device(): wide = lax.all_gather(wide, 'col')]
    ppermute x1 -> x33, waiting for transfers between devices: 0.01 us -> 63.6 us  [the longest x6 33.4 us: z_from0(): return lax.ppermute(value, 'col', [(b, 4 * s + b) for b in range(4)])]
    gather x10 -> x1, local copies, waits for them, and re-layouts: 33.4 us -> 0.64 us  [per_device(): jnp.take(index_map, jnp.maximum(held, 0))]
    another operation x36 -> x0, matrix products: 30 us -> none  [the longest x20 25.9 us: build_panel(): lax.linalg.triangular_solve(factor, panel_cols, left_side=False, lower=Tr...]
  transfers between devices with their start and end apart: 14 -> 34, of which waited for: 9 -> 10; matrix products, arithmetic and copies ran while one was open for 32% -> 6% of each run, Pallas kernels for 0% -> 26%
where the time goes in v1:
time: 286 us; the launch traced here: 282 us
  Pallas kernels  102 us (36%)
  starting transfers between devices  78.1 us (27%)
  waiting for transfers between devices  63.6 us (22%)
  other arithmetic  15.4 us (5%)
  between operations  14.2 us (5%)
  local copies, waits for them, and re-layouts  9.52 us (3%)
    pallas_call x4, Pallas kernels, panel_call(): pl.pallas_call(functools.partial(panel_kernel, k, base), out_shape=[jax.S...  72.4 us
    ppermute x5, starting transfers between devices, per_device(): thick.append(lax.ppermute(column, 'col', pairs))  44 us
    ppermute x6, waiting for transfers between devices, z_from0(): return lax.ppermute(value, 'col', [(b, 4 * s + b) for b in range(4)])  33.4 us
    pallas_call x1, Pallas kernels, tail_call(): pl.pallas_call(tail_kernel, out_shape=jax.ShapeDtypeStruct((LEAD, PANEL),...  29.2 us
    ppermute x3, waiting for transfers between devices, y_shift(): lax.ppermute(value, 'col', [(4 * z + b, 4 * z + (b + s) % 4) for z in ran...  21.2 us
    ppermute x12, starting transfers between devices, x_shift(): return lax.ppermute(value, 'row', [(i, (i + s) % 4) for i in range(4)])  17.6 us
    unnamed x53, local copies, waits for them, and re-layouts  8.55 us
    ppermute x6, starting transfers between devices, x_from0(): return lax.ppermute(value, grid, [(flat(0, c), flat(s, c)) for c in cols])  7.53 us
  transfers between devices with their start and end apart: 34, of which 10 were waited for; matrix products, arithmetic and copies ran while one was open for 6% of the time, Pallas kernels for 26%

profile of v1, /device:TPU:46, one launch (start us, length us, event | category | flops | bytes accessed | tf_op | source)
XLA Modules:
  0.0 282.4 jit_solution(15439256074114822594)
XLA Ops:
  6.5 1.6 collective-permute-done.3
  8.6 2.4 collective-permute-start.5
  11.0 1.8 bitcast_convert_fusion.1
  12.8 1.6 collective-permute-done.4
  14.4 1.9 collective-permute-done.5
  16.3 1.8 collective-permute-done.6
  18.4 1.0 fusion.7
  19.4 1.3 collective-permute-start.7
  20.7 0.7 collective-permute-start.8
  21.4 1.4 collective-permute-start.9
  22.8 10.7 %collective-permute-done.7 = bf16[384,512]{1,0:T(8,128)(2,1)S(1)} collective-permute-done((bf16[384,512]{1,0:T(8,128)(2,1)}, bf16[384,512]{1,0:T(8,128)(2,1)S(1)}, u32[]{:S(2)}, u32[]{:S(2)}) %collective-permute-start.7) | collective-permute-done | bytes 393248 | tf_op jit(solution)/shard_map/ppermute | solution.py:420
  33.5 2.0 fusion.6
  35.6 1.3 fusion
  36.9 0.7 slice_dynamic-update-slice_fusion.19
  37.6 0.7 slice_dynamic-update-slice_fusion.18
  38.3 0.7 slice_dynamic-update-slice_fusion.17
  39.0 0.7 slice_dynamic-update-slice_fusion.16
  39.7 0.7 slice_dynamic-update-slice_fusion.15
  40.4 0.6 constant_dynamic-update-slice_fusion.1
  41.0 0.7 collective-permute-start.15
  41.7 0.6 constant_dynamic-update-slice_fusion.2
  42.3 0.7 collective-permute-start.16
  43.0 0.6 constant_dynamic-update-slice_fusion.3
  43.6 1.4 collective-permute-start.17
  45.0 1.8 collective-permute-start
  46.7 1.7 collective-permute-start.1
  48.5 1.3 collective-permute-start.2
  49.8 1.1 add_add_fusion.2
  50.9 1.3 collective-permute-start.18
  52.3 0.7 collective-permute-start.19
  52.9 22.7 %collective-permute-done.18 = bf16[512,384]{1,0:T(8,128)(2,1)S(1)} collective-permute-done((bf16[512,384]{1,0:T(8,128)(2,1)S(1)}, bf16[512,384]{1,0:T(8,128)(2,1)S(1)}, u32[]{:S(2)}, u32[]{:S(2)}) %collective-permute-start.18) | collective-permute-done | bytes 393248 | tf_op jit(solution)/shard_map/ppermute | solution.py:420
  75.7 1.4 collective-permute-start.20
  77.0 0.7 maximum_bitcast_fusion
  77.8 0.6 gather_fusion
  78.4 0.7 bitcast_select_fusion.1
  79.2 0.7 collective-permute-start.10
  79.9 28.4 %collective-permute-start.11 = (bf16[2048,128]{1,0:T(8,128)(2,1)S(1)}, bf16[2048,128]{1,0:T(8,128)(2,1)S(1)}, u32[]{:S(2)}, u32[]{:S(2)}) collective-permute-start(bf16[2048,128]{1,0:T(8,128)(2,1)S(1)} %pad_maximum_fusion.3), channel_id=1, source_target_pairs={{4,11},{5,12},{8,13},{11,14},{14,15},{20,27},{21,28},{24,29},{27,3... | collective-permute-start | bytes 1572872 | tf_op jit(solution)/shard_map/ppermute | solution.py:470
  108.3 1.1 add_add_fusion.1
  109.6 2.0 collective-permute-start.23
  111.6 3.3 %add_add_fusion.a12 = bf16[1536,384]{1,0:T(8,128)(2,1)} fusion(bf16[1536,384]{1,0:T(8,128)(2,1)} %collective-permute-done.2, bf16[1536,384]{1,0:T(8,128)(2,1)} %collective-permute-done, bf16[1536,384]{1,0:T(8,128)(2,1)} %collective-permute-done.1), kind=kLoop, calls=%fused_computation.8 | loop fusion | flops 1179648 | bytes 4718592 | tf_op jit(solution)/shard_map/add | solution.py:480
  114.9 8.1 %collective-permute-done.21 = bf16[512,384]{1,0:T(8,128)(2,1)S(1)} collective-permute-done((bf16[512,384]{1,0:T(8,128)(2,1)S(1)}, bf16[512,384]{1,0:T(8,128)(2,1)S(1)}, u32[]{:S(2)}, u32[]{:S(2)}) %collective-permute-start.21) | collective-permute-done | bytes 393248 | tf_op jit(solution)/shard_map/ppermute | solution.py:426
  123.0 8.9 %collective-permute-done.22 = bf16[512,384]{1,0:T(8,128)(2,1)S(1)} collective-permute-done((bf16[512,384]{1,0:T(8,128)(2,1)S(1)}, bf16[512,384]{1,0:T(8,128)(2,1)S(1)}, u32[]{:S(2)}, u32[]{:S(2)}) %collective-permute-start.22) | collective-permute-done | bytes 393248 | tf_op jit(solution)/shard_map/ppermute | solution.py:426
  131.9 4.2 %collective-permute-done.23 = bf16[512,384]{1,0:T(8,128)(2,1)S(1)} collective-permute-done((bf16[512,384]{1,0:T(8,128)(2,1)S(1)}, bf16[512,384]{1,0:T(8,128)(2,1)S(1)}, u32[]{:S(2)}, u32[]{:S(2)}) %collective-permute-start.23) | collective-permute-done | bytes 393248 | tf_op jit(solution)/shard_map/ppermute | solution.py:426
  136.5 0.8 collective-permute-start.24
  137.2 3.1 %collective-permute-start.25 = (bf16[288,384]{1,0:T(8,128)(2,1)S(1)}, bf16[288,384]{1,0:T(8,128)(2,1)S(1)}, u32[]{:S(2)}, u32[]{:S(2)}) collective-permute-start(bf16[288,384]{1,0:T(8,128)(2,1)S(1)} %pad_maximum_fusion.5.refs_0_.refs_4_.refs_5_), channel_id=1, source_target_pairs={{0,32},{16,48},{32,0},{48,16},{1,33},{17,49},{33,1},{49,17},{2,34}... | collective-permute-start | bytes 663560 | tf_op jit(solution)/shard_map/ppermute | solution.py:423
  140.5 2.0 collective-permute-done.24.refs_1_.refs_5_.refs_6_
  142.5 2.5 collective-permute-start.27
  145.0 3.9 %collective-permute-start.28 = (bf16[288,384]{1,0:T(8,128)(2,1)S(1)}, bf16[288,384]{1,0:T(8,128)(2,1)S(1)}, u32[]{:S(2)}, u32[]{:S(2)}) collective-permute-start(bf16[288,384]{1,0:T(8,128)(2,1)S(1)} %dynamic-slice_bitcast_fusion.2.refs_0_), channel_id=1, source_target_pairs={{0,32},{16,48},{32,0},{48,16},{1,33},{17,49},{33,1},{49,17},{2,34}... | collective-permute-start | bytes 663560 | tf_op jit(solution)/shard_map/ppermute | solution.py:423
  148.9 14.0 %panel0.1 = (bf16[384,384]{1,0:T(8,128)(2,1)S(1)}, bf16[384,384]{1,0:T(8,128)(2,1)S(1)}, bf16[16,384]{1,0:T(8,128)(2,1)S(1)}, f32[384,384]{1,0:T(8,128)S(1)}, f32[384,384]{1,0:T(8,128)}) custom-call(s32[16]{0:T(128)S(1)} %concatenate.81.info, s32[16]{0:T(128)S(1)} %bitcast.55, bf16[288,384]{1,0:T(8,128)(2,1)S(1)} %pad_maximum_fusion.5.refs_0_.refs_4_.refs_5_, ...), custom_call_target="tpu_custom_call" | custom-call | flops 10000000000 | bytes 1000000 | tf_op jit(solution)/shard_map/panel0/pallas_call | solution.py:199
  162.9 3.3 %collective-permute-start.30 = (bf16[864,384]{1,0:T(8,128)(2,1)S(1)}, bf16[864,384]{1,0:T(8,128)(2,1)S(1)}, u32[]{:S(2)}, u32[]{:S(2)}) collective-permute-start(bf16[864,384]{1,0:T(8,128)(2,1)S(1)} %pad_maximum_fusion.1.refs_0_), channel_id=1, source_target_pairs={{0,16},{16,32},{32,48},{48,0},{1,17},{17,33},{33,49},{49,1},{2,18}... | collective-permute-start | bytes 1990664 | tf_op jit(solution)/shard_map/ppermute | solution.py:423
  166.2 1.2 collective-permute-start.32
  167.3 14.5 %panel1.1 = (bf16[384,384]{1,0:T(8,128)(2,1)S(1)}, bf16[384,384]{1,0:T(8,128)(2,1)S(1)}, bf16[384,384]{1,0:T(8,128)(2,1)S(1)}, f32[384,384]{1,0:T(8,128)S(1)}, f32[384,384]{1,0:T(8,128)S(1)}) custom-call(s32[16]{0:T(128)S(1)} %concatenate.81.info, s32[16]{0:T(128)S(1)} %bitcast.56, bf16[288,384]{1,0:T(8,128)(2,1)S(1)} %dynamic-slice_bitcast_fusion.2.refs_0_, ...), custom_call_target="tpu_custom_call" | custom-call | flops 10000000000 | bytes 1000000 | tf_op jit(solution)/shard_map/panel1/pallas_call | solution.py:199
  181.9 12.8 %collective-permute-start.12 = (bf16[2048,128]{1,0:T(8,128)(2,1)S(1)}, bf16[2048,128]{1,0:T(8,128)(2,1)S(1)}, u32[]{:S(2)}, u32[]{:S(2)}) collective-permute-start(bf16[2048,128]{1,0:T(8,128)(2,1)S(1)} %pad_maximum_fusion.3), channel_id=1, source_target_pairs={{5,11},{6,12},{9,13},{12,14},{15,15},{21,27},{22,28},{25,29},{28,3... | collective-permute-start | bytes 1572872 | tf_op jit(solution)/shard_map/ppermute | solution.py:470
  194.8 0.7 collective-permute-start.13
  195.5 1.5 collective-permute-start.14
  197.0 15.8 %panel2.1 = (bf16[384,384]{1,0:T(8,128)(2,1)S(1)}, bf16[384,384]{1,0:T(8,128)(2,1)S(1)}, bf16[768,384]{1,0:T(8,128)(2,1)S(1)}, f32[384,384]{1,0:T(8,128)S(1)}, f32[384,384]{1,0:T(8,128)S(1)}) custom-call(s32[16]{0:T(128)S(1)} %concatenate.81.info, s32[16]{0:T(128)S(1)} %bitcast.57, bf16[864,384]{1,0:T(8,128)(2,1)S(1)} %pad_maximum_fusion.1.refs_0_, ...), custom_call_target="tpu_custom_call" | custom-call | flops 10000000000 | bytes 1000000 | tf_op jit(solution)/shard_map/panel2/pallas_call | solution.py:199
  212.9 28.1 %panel3.1 = (bf16[384,384]{1,0:T(8,128)(2,1)S(1)}, bf16[384,384]{1,0:T(8,128)(2,1)}, bf16[1152,384]{1,0:T(8,128)(2,1)S(1)}, f32[384,384]{1,0:T(8,128)S(1)}, f32[384,384]{1,0:T(8,128)S(1)}) custom-call(s32[16]{0:T(128)S(1)} %concatenate.81.info, s32[16]{0:T(128)S(1)} %bitcast.58, bf16[864,384]{1,0:T(8,128)(2,1)S(1)} %pad_maximum_fusion.1.refs_0_, ...), custom_call_target="tpu_custom_call" | custom-call | flops 10000000000 | bytes 1000000 | tf_op jit(solution)/shard_map/panel3/pallas_call | solution.py:199
  241.1 1.0 copy-done.6
  242.0 0.8 copy-done.13
  242.9 0.8 copy-done.14
  243.7 0.7 copy-done.19
  244.4 0.7 copy-done.20
  245.5 0.6 copy-done.23
  246.2 29.2 %tail.1 = f32[1536,384]{1,0:T(8,128)} custom-call(s32[16]{0:T(128)} %copy-done.2, s32[16]{0:T(128)} %bitcast.53, f32[1536,384]{1,0:T(8,128)} %bitcast.59, bf16[1536,384]{1,0:T(8,128)(2,1)} %add_add_fusion.a12, bf16[16,384,512]{2,1,0:T(8,128)(2,1)} %bitcast.68, bf16[2048,128]{1,0:T(8,128)(2,1)} %copy-done.20, bf16[2048,128]{1,0:T(8,128)(2,1)} %copy-done.21, ...), custom_call_target="tpu_custom_call" | custom-call | flops 7000000000 | bytes 20000000 | tf_op jit(solution)/shard_map/tail/pallas_call | solution.py:389
  (94 shorter events, 2.0 us)
Async XLA Ops:
  6.5 238.8 %all-gather.3.cloned.1.call-start = ((), (), s32[]{:S(2)}) async-start(), calls=%async_computation | async-start | bytes 6684672 | tf_op jit(solution)/shard_map/all_gather | solution.py:476
  6.5 1.6 collective-permute-start.3
  8.1 6.3 %collective-permute-start.4 = (bf16[512,128]{1,0:T(8,128)(2,1)S(1)}, bf16[512,128]{1,0:T(8,128)(2,1)S(1)}, u32[]{:S(2)}, u32[]{:S(2)}) collective-permute-start(bf16[512,128]{1,0:T(8,128)(2,1)S(1)} %collective-permute-done.3), channel_id=1, source_target_pairs={{0,16},{16,32},{32,48},{48,0},{1,17},{17,33},{33,49},{49,1},{2,18}... | collective-permute-start | bytes 393224 | tf_op jit(solution)/shard_map/ppermute | solution.py:423
  8.6 7.7 %collective-permute-start.5 = (bf16[512,128]{1,0:T(8,128)(2,1)S(1)}, bf16[512,128]{1,0:T(8,128)(2,1)S(1)}, u32[]{:S(2)}, u32[]{:S(2)}) collective-permute-start(bf16[512,128]{1,0:T(8,128)(2,1)S(1)} %collective-permute-done.3), channel_id=1, source_target_pairs={{0,32},{16,48},{32,0},{48,16},{1,33},{17,49},{33,1},{49,17},{2,34}... | collective-permute-start | bytes 393224 | tf_op jit(solution)/shard_map/ppermute | solution.py:423
  11.0 7.2 %collective-permute-start.6 = (bf16[512,128]{1,0:T(8,128)(2,1)S(1)}, bf16[512,128]{1,0:T(8,128)(2,1)S(1)}, u32[]{:S(2)}, u32[]{:S(2)}) collective-permute-start(bf16[512,128]{1,0:T(8,128)(2,1)S(1)} %collective-permute-done.3), channel_id=1, source_target_pairs={{0,48},{16,0},{32,16},{48,32},{1,49},{17,1},{33,17},{49,33},{2,50}... | collective-permute-start | bytes 393224 | tf_op jit(solution)/shard_map/ppermute | solution.py:423
  19.4 14.1 %collective-permute-start.7 = (bf16[384,512]{1,0:T(8,128)(2,1)}, bf16[384,512]{1,0:T(8,128)(2,1)S(1)}, u32[]{:S(2)}, u32[]{:S(2)}) collective-permute-start(bf16[384,512]{1,0:T(8,128)(2,1)} %get-tuple-element.318), channel_id=1, source_target_pairs={{0,4},{1,5},{2,6},{3,7},{16,20},{17,21},{18,22},{19,23},{32,36},{3... | collective-permute-start | bytes 1179656 | tf_op jit(solution)/shard_map/ppermute | solution.py:420
  20.7 12.9 %collective-permute-start.8 = (bf16[384,512]{1,0:T(8,128)(2,1)}, bf16[384,512]{1,0:T(8,128)(2,1)S(1)}, u32[]{:S(2)}, u32[]{:S(2)}) collective-permute-start(bf16[384,512]{1,0:T(8,128)(2,1)} %get-tuple-element.320), channel_id=1, source_target_pairs={{0,8},{1,9},{2,10},{3,11},{16,24},{17,25},{18,26},{19,27},{32,40},... | collective-permute-start | bytes 1179656 | tf_op jit(solution)/shard_map/ppermute | solution.py:420
  21.4 12.2 %collective-permute-start.9 = (bf16[384,512]{1,0:T(8,128)(2,1)S(1)}, bf16[384,512]{1,0:T(8,128)(2,1)}, u32[]{:S(2)}, u32[]{:S(2)}) collective-permute-start(bf16[384,512]{1,0:T(8,128)(2,1)S(1)} %get-tuple-element.319), channel_id=1, source_target_pairs={{0,12},{1,13},{2,14},{3,15},{16,28},{17,29},{18,30},{19,31},{32,44... | collective-permute-start | bytes 1179656 | tf_op jit(solution)/shard_map/ppermute | solution.py:420
  39.7 38.1 %copy-start = (s32[1,16]{1,0:T(1,128)S(1)}, s32[1,16]{1,0:T(1,128)}, u32[]{:S(2)}) copy-start(s32[1,16]{1,0:T(1,128)} %param.47) | copy-start | bytes 196
  41.0 7.5 %collective-permute-start.15 = (bf16[512,384]{1,0:T(8,128)(2,1)}, bf16[512,384]{1,0:T(8,128)(2,1)S(1)}, u32[]{:S(2)}, u32[]{:S(2)}) collective-permute-start(bf16[512,384]{1,0:T(8,128)(2,1)} %constant_dynamic-update-slice_fusion.1), channel_id=1, source_target_pairs={{0,16},{1,17},{2,18},{3,19},{64,80},{65,81},{66,82},{67,83}} | collective-permute-start | bytes 1179656 | tf_op jit(solution)/shard_map/ppermute | solution.py:417
  42.3 7.5 %collective-permute-start.16 = (bf16[512,384]{1,0:T(8,128)(2,1)}, bf16[512,384]{1,0:T(8,128)(2,1)S(1)}, u32[]{:S(2)}, u32[]{:S(2)}) collective-permute-start(bf16[512,384]{1,0:T(8,128)(2,1)} %constant_dynamic-update-slice_fusion.2), channel_id=1, source_target_pairs={{0,32},{1,33},{2,34},{3,35},{64,96},{65,97},{66,98},{67,99}} | collective-permute-start | bytes 1179656 | tf_op jit(solution)/shard_map/ppermute | solution.py:417
  43.6 6.2 %collective-permute-start.17 = (bf16[512,384]{1,0:T(8,128)(2,1)}, bf16[512,384]{1,0:T(8,128)(2,1)}, u32[]{:S(2)}, u32[]{:S(2)}) collective-permute-start(bf16[512,384]{1,0:T(8,128)(2,1)} %constant_dynamic-update-slice_fusion.3), channel_id=1, source_target_pairs={{0,48},{1,49},{2,50},{3,51},{64,112},{65,113},{66,114},{67,115}} | collective-permute-start | bytes 1179656 | tf_op jit(solution)/shard_map/ppermute | solution.py:417
  45.0 64.4 %collective-permute-start = (bf16[1536,384]{1,0:T(8,128)(2,1)S(1)}, bf16[1536,384]{1,0:T(8,128)(2,1)}, u32[]{:S(2)}, u32[]{:S(2)}) collective-permute-start(bf16[1536,384]{1,0:T(8,128)(2,1)S(1)} %bitcast_convert_fusion.1), channel_id=1, source_target_pairs={{4,20},{5,21},{6,22},{7,23},{8,24},{9,25},{10,26},{11,27},{12,28},... | collective-permute-start | bytes 3538952 | tf_op jit(solution)/shard_map/ppermute | solution.py:417
  46.7 62.8 %collective-permute-start.1 = (bf16[1536,384]{1,0:T(8,128)(2,1)S(1)}, bf16[1536,384]{1,0:T(8,128)(2,1)}, u32[]{:S(2)}, u32[]{:S(2)}) collective-permute-start(bf16[1536,384]{1,0:T(8,128)(2,1)S(1)} %bitcast_convert_fusion.1), channel_id=1, source_target_pairs={{4,36},{5,37},{6,38},{7,39},{8,40},{9,41},{10,42},{11,43},{12,44},... | collective-permute-start | bytes 3538952 | tf_op jit(solution)/shard_map/ppermute | solution.py:417
  48.5 61.1 %collective-permute-start.2 = (bf16[1536,384]{1,0:T(8,128)(2,1)S(1)}, bf16[1536,384]{1,0:T(8,128)(2,1)}, u32[]{:S(2)}, u32[]{:S(2)}) collective-permute-start(bf16[1536,384]{1,0:T(8,128)(2,1)S(1)} %bitcast_convert_fusion.1), channel_id=1, source_target_pairs={{4,52},{5,53},{6,54},{7,55},{8,56},{9,57},{10,58},{11,59},{12,60},... | collective-permute-start | bytes 3538952 | tf_op jit(solution)/shard_map/ppermute | solution.py:417
  50.9 24.7 %collective-permute-start.18 = (bf16[512,384]{1,0:T(8,128)(2,1)S(1)}, bf16[512,384]{1,0:T(8,128)(2,1)S(1)}, u32[]{:S(2)}, u32[]{:S(2)}) collective-permute-start(bf16[512,384]{1,0:T(8,128)(2,1)S(1)} %add_add_fusion.2), channel_id=1, source_target_pairs={{0,4},{1,5},{2,6},{3,7},{16,20},{17,21},{18,22},{19,23},{32,36},{3... | collective-permute-start | bytes 1179656 | tf_op jit(solution)/shard_map/ppermute | solution.py:420
  52.3 26.9 %collective-permute-start.19 = (bf16[512,384]{1,0:T(8,128)(2,1)S(1)}, bf16[512,384]{1,0:T(8,128)(2,1)S(1)}, u32[]{:S(2)}, u32[]{:S(2)}) collective-permute-start(bf16[512,384]{1,0:T(8,128)(2,1)S(1)} %add_add_fusion.2), channel_id=1, source_target_pairs={{0,8},{1,9},{2,10},{3,11},{16,24},{17,25},{18,26},{19,27},{32,40},... | collective-permute-start | bytes 1179656 | tf_op jit(solution)/shard_map/ppermute | solution.py:420
  75.7 4.3 %collective-permute-start.20 = (bf16[512,384]{1,0:T(8,128)(2,1)S(1)}, bf16[512,384]{1,0:T(8,128)(2,1)}, u32[]{:S(2)}, u32[]{:S(2)}) collective-permute-start(bf16[512,384]{1,0:T(8,128)(2,1)S(1)} %add_add_fusion.2), channel_id=1, source_target_pairs={{0,12},{1,13},{2,14},{3,15},{16,28},{17,29},{18,30},{19,31},{32,44... | collective-permute-start | bytes 1179656 | tf_op jit(solution)/shard_map/ppermute | solution.py:420
  79.2 133.6 %copy-start.2 = (s32[16]{0:T(128)}, s32[16]{0:T(128)S(1)}, u32[]{:S(2)}) copy-start(s32[16]{0:T(128)S(1)} %concatenate.81.info) | copy-start | bytes 196
  79.2 165.2 %collective-permute-start.10 = (bf16[2048,128]{1,0:T(8,128)(2,1)S(1)}, bf16[2048,128]{1,0:T(8,128)(2,1)S(1)}, u32[]{:S(2)}, u32[]{:S(2)}) collective-permute-start(bf16[2048,128]{1,0:T(8,128)(2,1)S(1)} %pad_maximum_fusion.3), channel_id=1, source_target_pairs={{3,11},{4,12},{7,13},{10,14},{13,15},{19,27},{20,28},{23,29},{26,3... | collective-permute-start | bytes 1572872 | tf_op jit(solution)/shard_map/ppermute | solution.py:470
  79.9 164.5 %collective-permute-start.11 = (bf16[2048,128]{1,0:T(8,128)(2,1)S(1)}, bf16[2048,128]{1,0:T(8,128)(2,1)S(1)}, u32[]{:S(2)}, u32[]{:S(2)}) collective-permute-start(bf16[2048,128]{1,0:T(8,128)(2,1)S(1)} %pad_maximum_fusion.3), channel_id=1, source_target_pairs={{4,11},{5,12},{8,13},{11,14},{14,15},{20,27},{21,28},{24,29},{27,3... | collective-permute-start | bytes 1572872 | tf_op jit(solution)/shard_map/ppermute | solution.py:470
  109.4 13.6 %collective-permute-start.21 = (bf16[512,384]{1,0:T(8,128)(2,1)S(1)}, bf16[512,384]{1,0:T(8,128)(2,1)S(1)}, u32[]{:S(2)}, u32[]{:S(2)}) collective-permute-start(bf16[512,384]{1,0:T(8,128)(2,1)S(1)} %add_add_fusion.1), channel_id=1, source_target_pairs={{0,1},{1,2},{2,3},{3,0},{4,5},{5,6},{6,7},{7,4},{8,9},{9,10},{10,1... | collective-permute-start | bytes 1179656 | tf_op jit(solution)/shard_map/ppermute | solution.py:426
  109.5 22.4 %collective-permute-start.22 = (bf16[512,384]{1,0:T(8,128)(2,1)S(1)}, bf16[512,384]{1,0:T(8,128)(2,1)S(1)}, u32[]{:S(2)}, u32[]{:S(2)}) collective-permute-start(bf16[512,384]{1,0:T(8,128)(2,1)S(1)} %add_add_fusion.1), channel_id=1, source_target_pairs={{0,2},{1,3},{2,0},{3,1},{4,6},{5,7},{6,4},{7,5},{8,10},{9,11},{10,... | collective-permute-start | bytes 1179656 | tf_op jit(solution)/shard_map/ppermute | solution.py:426
  109.6 26.5 %collective-permute-start.23 = (bf16[512,384]{1,0:T(8,128)(2,1)S(1)}, bf16[512,384]{1,0:T(8,128)(2,1)S(1)}, u32[]{:S(2)}, u32[]{:S(2)}) collective-permute-start(bf16[512,384]{1,0:T(8,128)(2,1)S(1)} %add_add_fusion.1), channel_id=1, source_target_pairs={{0,3},{1,0},{2,1},{3,2},{4,7},{5,4},{6,5},{7,6},{8,11},{9,8},{10,9... | collective-permute-start | bytes 1179656 | tf_op jit(solution)/shard_map/ppermute | solution.py:426
  136.5 76.4 %copy-start.1 = (bf16[288,384]{1,0:T(8,128)(2,1)}, bf16[288,384]{1,0:T(8,128)(2,1)S(1)}, u32[]{:S(2)}) copy-start(bf16[288,384]{1,0:T(8,128)(2,1)S(1)} %pad_maximum_fusion.5.refs_0_.refs_4_.refs_5_) | copy-start | bytes 663556
  136.5 6.0 %collective-permute-start.24 = (bf16[288,384]{1,0:T(8,128)(2,1)S(1)}, bf16[288,384]{1,0:T(8,128)(2,1)S(1)}, u32[]{:S(2)}, u32[]{:S(2)}) collective-permute-start(bf16[288,384]{1,0:T(8,128)(2,1)S(1)} %pad_maximum_fusion.5.refs_0_.refs_4_.refs_5_), channel_id=1, source_target_pairs={{0,16},{16,32},{32,48},{48,0},{1,17},{17,33},{33,49},{49,1},{2,18}... | collective-permute-start | bytes 663560 | tf_op jit(solution)/shard_map/ppermute | solution.py:423
  137.2 7.7 %collective-permute-start.25 = (bf16[288,384]{1,0:T(8,128)(2,1)S(1)}, bf16[288,384]{1,0:T(8,128)(2,1)S(1)}, u32[]{:S(2)}, u32[]{:S(2)}) collective-permute-start(bf16[288,384]{1,0:T(8,128)(2,1)S(1)} %pad_maximum_fusion.5.refs_0_.refs_4_.refs_5_), channel_id=1, source_target_pairs={{0,32},{16,48},{32,0},{48,16},{1,33},{17,49},{33,1},{49,17},{2,34}... | collective-permute-start | bytes 663560 | tf_op jit(solution)/shard_map/ppermute | solution.py:423
  140.3 8.6 %collective-permute-start.26 = (bf16[288,384]{1,0:T(8,128)(2,1)S(1)}, bf16[288,384]{1,0:T(8,128)(2,1)S(1)}, u32[]{:S(2)}, u32[]{:S(2)}) collective-permute-start(bf16[288,384]{1,0:T(8,128)(2,1)S(1)} %pad_maximum_fusion.5.refs_0_.refs_4_.refs_5_), channel_id=1, source_target_pairs={{0,48},{16,0},{32,16},{48,32},{1,49},{17,1},{33,17},{49,33},{2,50}... | collective-permute-start | bytes 663560 | tf_op jit(solution)/shard_map/ppermute | solution.py:423
  142.5 70.4 %copy-start.3 = (bf16[288,384]{1,0:T(8,128)(2,1)}, bf16[288,384]{1,0:T(8,128)(2,1)S(1)}, u32[]{:S(2)}) copy-start(bf16[288,384]{1,0:T(8,128)(2,1)S(1)} %collective-permute-done.24.refs_1_.refs_5_.refs_6_) | copy-start | bytes 663556
  142.5 20.4 %collective-permute-start.27 = (bf16[288,384]{1,0:T(8,128)(2,1)S(1)}, bf16[288,384]{1,0:T(8,128)(2,1)S(1)}, u32[]{:S(2)}, u32[]{:S(2)}) collective-permute-start(bf16[288,384]{1,0:T(8,128)(2,1)S(1)} %dynamic-slice_bitcast_fusion.2.refs_0_), channel_id=1, source_target_pairs={{0,16},{16,32},{32,48},{48,0},{1,17},{17,33},{33,49},{49,1},{2,18}... | collective-permute-start | bytes 663560 | tf_op jit(solution)/shard_map/ppermute | solution.py:423
  145.0 67.9 %copy-start.4 = (bf16[288,384]{1,0:T(8,128)(2,1)}, bf16[288,384]{1,0:T(8,128)(2,1)S(1)}, u32[]{:S(2)}) copy-start(bf16[288,384]{1,0:T(8,128)(2,1)S(1)} %collective-permute-done.25.refs_2_.refs_6_.refs_7_) | copy-start | bytes 663556
  145.0 21.2 %collective-permute-start.28 = (bf16[288,384]{1,0:T(8,128)(2,1)S(1)}, bf16[288,384]{1,0:T(8,128)(2,1)S(1)}, u32[]{:S(2)}, u32[]{:S(2)}) collective-permute-start(bf16[288,384]{1,0:T(8,128)(2,1)S(1)} %dynamic-slice_bitcast_fusion.2.refs_0_), channel_id=1, source_target_pairs={{0,32},{16,48},{32,0},{48,16},{1,33},{17,49},{33,1},{49,17},{2,34}... | collective-permute-start | bytes 663560 | tf_op jit(solution)/shard_map/ppermute | solution.py:423
  148.8 64.0 %copy-start.5 = (bf16[288,384]{1,0:T(8,128)(2,1)}, bf16[288,384]{1,0:T(8,128)(2,1)S(1)}, u32[]{:S(2)}) copy-start(bf16[288,384]{1,0:T(8,128)(2,1)S(1)} %collective-permute-done.26.refs_3_.refs_7_.refs_8_) | copy-start | bytes 663556
  148.8 17.3 %collective-permute-start.29 = (bf16[288,384]{1,0:T(8,128)(2,1)S(1)}, bf16[288,384]{1,0:T(8,128)(2,1)S(1)}, u32[]{:S(2)}, u32[]{:S(2)}) collective-permute-start(bf16[288,384]{1,0:T(8,128)(2,1)S(1)} %dynamic-slice_bitcast_fusion.2.refs_0_), channel_id=1, source_target_pairs={{0,48},{16,0},{32,16},{48,32},{1,49},{17,1},{33,17},{49,33},{2,50}... | collective-permute-start | bytes 663560 | tf_op jit(solution)/shard_map/ppermute | solution.py:423
  162.8 19.0 %copy-start.7 = (f32[384,384]{1,0:T(8,128)}, f32[384,384]{1,0:T(8,128)S(1)}, u32[]{:S(2)}) copy-start(f32[384,384]{1,0:T(8,128)S(1)} %get-tuple-element.286.refs_16_) | copy-start | bytes 1769476
  162.8 50.0 %copy-start.15 = (bf16[384,384]{1,0:T(8,128)(2,1)}, bf16[384,384]{1,0:T(8,128)(2,1)S(1)}, u32[]{:S(2)}) copy-start(bf16[384,384]{1,0:T(8,128)(2,1)S(1)} %get-tuple-element.276.refs_9_.refs_10_.refs_11_.refs_12_) | copy-start | bytes 884740
  162.9 19.1 %collective-permute-start.30 = (bf16[864,384]{1,0:T(8,128)(2,1)S(1)}, bf16[864,384]{1,0:T(8,128)(2,1)S(1)}, u32[]{:S(2)}, u32[]{:S(2)}) collective-permute-start(bf16[864,384]{1,0:T(8,128)(2,1)S(1)} %pad_maximum_fusion.1.refs_0_), channel_id=1, source_target_pairs={{0,16},{16,32},{32,48},{48,0},{1,17},{17,33},{33,49},{49,1},{2,18}... | collective-permute-start | bytes 1990664 | tf_op jit(solution)/shard_map/ppermute | solution.py:423
  166.2 28.6 %collective-permute-start.31 = (bf16[864,384]{1,0:T(8,128)(2,1)S(1)}, bf16[864,384]{1,0:T(8,128)(2,1)S(1)}, u32[]{:S(2)}, u32[]{:S(2)}) collective-permute-start(bf16[864,384]{1,0:T(8,128)(2,1)S(1)} %pad_maximum_fusion.1.refs_0_), channel_id=1, source_target_pairs={{0,32},{16,48},{32,0},{48,16},{1,33},{17,49},{33,1},{49,17},{2,34}... | collective-permute-start | bytes 1990664 | tf_op jit(solution)/shard_map/ppermute | solution.py:423
  166.2 29.3 %collective-permute-start.32 = (bf16[864,384]{1,0:T(8,128)(2,1)S(1)}, bf16[864,384]{1,0:T(8,128)(2,1)S(1)}, u32[]{:S(2)}, u32[]{:S(2)}) collective-permute-start(bf16[864,384]{1,0:T(8,128)(2,1)S(1)} %pad_maximum_fusion.1.refs_0_), channel_id=1, source_target_pairs={{0,48},{16,0},{32,16},{48,32},{1,49},{17,1},{33,17},{49,33},{2,50}... | collective-permute-start | bytes 1990664 | tf_op jit(solution)/shard_map/ppermute | solution.py:423
  181.9 30.9 %copy-start.8 = (f32[384,384]{1,0:T(8,128)}, f32[384,384]{1,0:T(8,128)S(1)}, u32[]{:S(2)}) copy-start(f32[384,384]{1,0:T(8,128)S(1)} %get-tuple-element.287.refs_17_) | copy-start | bytes 1769476
  181.9 30.9 %copy-start.9 = (f32[384,384]{1,0:T(8,128)}, f32[384,384]{1,0:T(8,128)S(1)}, u32[]{:S(2)}) copy-start(f32[384,384]{1,0:T(8,128)S(1)} %get-tuple-element.290.refs_20_) | copy-start | bytes 1769476
  181.9 31.0 %copy-start.16 = (bf16[384,384]{1,0:T(8,128)(2,1)}, bf16[384,384]{1,0:T(8,128)(2,1)S(1)}, u32[]{:S(2)}) copy-start(bf16[384,384]{1,0:T(8,128)(2,1)S(1)} %get-tuple-element.279.refs_12_.refs_13_) | copy-start | bytes 884740
  181.9 31.0 %copy-start.17 = (bf16[384,384]{1,0:T(8,128)(2,1)}, bf16[384,384]{1,0:T(8,128)(2,1)S(1)}, u32[]{:S(2)}) copy-start(bf16[384,384]{1,0:T(8,128)(2,1)S(1)} %get-tuple-element.278.refs_9_) | copy-start | bytes 884740
  181.9 62.5 %collective-permute-start.12 = (bf16[2048,128]{1,0:T(8,128)(2,1)S(1)}, bf16[2048,128]{1,0:T(8,128)(2,1)S(1)}, u32[]{:S(2)}, u32[]{:S(2)}) collective-permute-start(bf16[2048,128]{1,0:T(8,128)(2,1)S(1)} %pad_maximum_fusion.3), channel_id=1, source_target_pairs={{5,11},{6,12},{9,13},{12,14},{15,15},{21,27},{22,28},{25,29},{28,3... | collective-permute-start | bytes 1572872 | tf_op jit(solution)/shard_map/ppermute | solution.py:470
  194.8 49.6 %collective-permute-start.13 = (bf16[2048,128]{1,0:T(8,128)(2,1)S(1)}, bf16[2048,128]{1,0:T(8,128)(2,1)S(1)}, u32[]{:S(2)}, u32[]{:S(2)}) collective-permute-start(bf16[2048,128]{1,0:T(8,128)(2,1)S(1)} %pad_maximum_fusion.3), channel_id=1, source_target_pairs={{7,12},{10,13},{13,14},{23,28},{26,29},{29,30},{39,44},{42,45},{45... | collective-permute-start | bytes 1572872 | tf_op jit(solution)/shard_map/ppermute | solution.py:470
  195.5 49.9 %collective-permute-start.14 = (bf16[2048,128]{1,0:T(8,128)(2,1)S(1)}, bf16[2048,128]{1,0:T(8,128)(2,1)}, u32[]{:S(2)}, u32[]{:S(2)}) collective-permute-start(bf16[2048,128]{1,0:T(8,128)(2,1)S(1)} %pad_maximum_fusion.3), channel_id=1, source_target_pairs={{8,12},{11,13},{14,14},{24,28},{27,29},{30,30},{40,44},{43,45},{46... | collective-permute-start | bytes 1572872 | tf_op jit(solution)/shard_map/ppermute | solution.py:470
  212.8 28.3 %copy-start.10 = (bf16[768,384]{1,0:T(8,128)(2,1)}, bf16[768,384]{1,0:T(8,128)(2,1)S(1)}, u32[]{:S(2)}) copy-start(bf16[768,384]{1,0:T(8,128)(2,1)S(1)} %get-tuple-element.281.refs_10_) | copy-start | bytes 1769476
  212.8 28.3 %copy-start.11 = (f32[384,384]{1,0:T(8,128)}, f32[384,384]{1,0:T(8,128)S(1)}, u32[]{:S(2)}) copy-start(f32[384,384]{1,0:T(8,128)S(1)} %get-tuple-element.288.refs_18_) | copy-start | bytes 1769476
  212.8 28.2 %copy-start.12 = (f32[384,384]{1,0:T(8,128)}, f32[384,384]{1,0:T(8,128)S(1)}, u32[]{:S(2)}) copy-start(f32[384,384]{1,0:T(8,128)S(1)} %get-tuple-element.291.refs_21_) | copy-start | bytes 1769476
  212.8 28.2 %copy-start.18 = (bf16[384,384]{1,0:T(8,128)(2,1)}, bf16[384,384]{1,0:T(8,128)(2,1)S(1)}, u32[]{:S(2)}) copy-start(bf16[384,384]{1,0:T(8,128)(2,1)S(1)} %get-tuple-element.282.refs_15_.refs_14_) | copy-start | bytes 884740
  241.0 1.0 copy-start.6
  242.0 0.8 copy-start.13
  242.9 0.8 copy-start.14
  243.7 0.7 copy-start.19
  244.4 0.8 copy-start.20
  244.4 1.0 copy-start.21
  244.4 1.1 copy-start.22
  245.4 0.8 copy-start.23
Sparse Core Ops, SparseCore 0:
  35.7 97.4 all-gather.2

commit v2 on v1

--- a/solution.py
+++ b/solution.py
@@ -13,6 +13,8 @@
 N_ROW = 4
 N_COL = 16
 PIECE = PANEL // N_ROW
+PART = BLK // N_ROW
+DIAG = 4 * PART
 LEAD = PANEL * PANELS
 F32 = jnp.float32
 BF16 = jnp.bfloat16
@@ -117,6 +119,15 @@
     lax.fori_loop(0, 3, step, 0)
 
 
+def unpack_child(t, piece, x):
+    at = pl.multiple_of(x * PIECE, 16)
+    for b in range(3):
+        for u in range(3):
+            t[pl.ds(at + PART * u, PART), b * BLK : (b + 1) * BLK] = piece[
+                DIAG + PART * b : DIAG + PART * (b + 1), u * BLK : (u + 1) * BLK
+            ].astype(F32)
+
+
 def panel_kernel(k, base, info, maps, *refs):
     r = list(refs)
     pieces, r = r[:4], r[4:]
@@ -128,18 +139,18 @@
     me = info[0]
     col = info[1]
     for s in range(4):
-        at = pl.multiple_of(lax.rem(me + 4 - s, 4) * PIECE, PIECE)
+        x = lax.rem(me + 4 - s, 4)
         buf = pieces[s]
         for j in range(k):
-            a[pl.ds(j * PANEL + at, PIECE), :] = buf[base + (2 + j) * PIECE : base + (3 + j) * PIECE, :].astype(F32)
-        a[pl.ds(k * PANEL + at, PIECE), :] = buf[base : base + PIECE, :].astype(F32) + buf[
-            base + PIECE : base + 2 * PIECE, :
-        ].astype(F32)
-        for b in range(3):
-            for u in range(3):
-                t[pl.ds(at + 32 * u, 32), b * BLK : (b + 1) * BLK] = t_pieces[s][
-                    2 * PIECE + 32 * b : 2 * PIECE + 32 * b + 32, u * BLK : (u + 1) * BLK
-                ].astype(F32)
+            at = pl.multiple_of(j * PANEL + x * PIECE, 16)
+            a[pl.ds(at, PIECE), :] = buf[base + DIAG + j * PIECE : base + DIAG + (j + 1) * PIECE, :].astype(F32)
+        at = pl.multiple_of(x * PART, PART)
+        first = buf[base : base + PART, :].astype(F32) + buf[base + 2 * PART : base + 3 * PART, :].astype(F32)
+        rest = buf[base + PART : base + 2 * PART, :].astype(F32) + buf[base + 3 * PART : base + 4 * PART, :].astype(F32)
+        a[pl.ds(k * PANEL + at, PART), :] = first
+        a[pl.ds(k * PANEL + BLK + at, PART), BLK:] = rest[:, : 2 * BLK]
+        a[pl.ds(k * PANEL + 2 * BLK + at, PART), 2 * BLK :] = rest[:, 2 * BLK :]
+        unpack_child(t, t_pieces[s], x)
     for b in range(3):
         mb = maps[b] - 3 * k
         for i in range(3):
@@ -275,12 +286,7 @@
             x[...] = a12[...].astype(F32)
 
         for s in range(4):
-            at = pl.multiple_of(lax.rem(me + 4 - s, 4) * PIECE, PIECE)
-            for b in range(3):
-                for u in range(3):
-                    t[pl.ds(at + 32 * u, 32), blk(b)] = t_pieces[s][
-                        2 * PIECE + 32 * b : 2 * PIECE + 32 * b + 32, blk(u)
-                    ].astype(F32)
+            unpack_child(t, t_pieces[s], lax.rem(me + 4 - s, 4))
         for i in range(3):
             ma = maps[i]
             for b in range(3):
@@ -425,60 +431,69 @@
     def y_shift(value, s):
         return lax.ppermute(value, "col", [(4 * z + b, 4 * z + (b + s) % 4) for z in range(4) for b in range(4)])
 
+    def after(value, *marks):
+        return lax.optimization_barrier((value, *marks))[0]
+
+    def own_or(root, value, *got):
+        out = jnp.where(root, value, jnp.zeros((), BF16))
+        for g in got:
+            out = out + g
+        return out
+
+    def by_source(value, shift, index, order):
+        around = jnp.stack([value] + [shift(value, s) for s in range(1, 4)])
+        return [lax.dynamic_index_in_dim(around, lax.rem(index + 4 - k, 4), 0, keepdims=False) for k in order]
+
     received = lax.ppermute(contribution[0], "cube", [(0, 1), (1, 0)])
-
     high = front.astype(BF16)
     diag = lax.dynamic_slice_in_dim(front, y * PANEL, PANEL, 0)
-    diag_high = diag.astype(BF16)
-    diag_low = (diag - diag_high.astype(F32)).astype(BF16)
-
-    def quarter(s):
-        rows = slice(s * PIECE, (s + 1) * PIECE)
-        child = received[rows, :]
-        child = jnp.concatenate([child[:32], child[32:64], child[64:96]], axis=1)
+
+    def diag_part(s):
+        a = diag[s * PART : (s + 1) * PART]
+        b = diag[BLK + s * PART : BLK + (s + 1) * PART, BLK:]
+        c = diag[2 * BLK + s * PART : 2 * BLK + (s + 1) * PART, 2 * BLK :]
+        rows = jnp.concatenate([a, jnp.concatenate([b, c], axis=1)], axis=0)
+        upper = rows.astype(BF16)
+        return [upper, (rows - upper.astype(F32)).astype(BF16)]
+
+    def child_part(s):
+        child = received[s * PIECE : (s + 1) * PIECE]
+        return jnp.concatenate([child[:PART], child[PART : 2 * PART], child[2 * PART :]], axis=1)
+
+    def rest_part(s):
         offs = [high[j * PANEL + s * PIECE : j * PANEL + (s + 1) * PIECE] for j in range(3)]
-        return jnp.concatenate([diag_high[rows], diag_low[rows], *offs, child], axis=0)
-
-    mine = jnp.where(me == 0, quarter(0), jnp.zeros((), BF16))
-    for s in range(1, 4):
-        mine = mine + x_from0(quarter(s), s, range(4))
-    at_root = mine
-    spread = jnp.where(col < 4, at_root, jnp.zeros((), BF16))
-    for s in range(1, 4):
-        spread = spread + z_from0(at_root, s)
-    around = [spread] + [y_shift(spread, s) for s in range(1, 4)]
-    stacked = jnp.stack(around)
-    order = [lax.rem(y + 4 - k, 4) for k in range(4)]
-    by_panel = [lax.dynamic_index_in_dim(stacked, order[k], 0, keepdims=False) for k in range(4)]
-    r0 = jnp.concatenate([by_panel[0][: 2 * PIECE]] + [by_panel[b][5 * PIECE :] for b in range(3)], axis=0)
-    r1 = by_panel[1][: 3 * PIECE]
-    r23 = jnp.concatenate([by_panel[2][: 4 * PIECE], by_panel[3][: 5 * PIECE]], axis=0)
-    g0 = [r0] + [x_shift(r0, s) for s in range(1, 4)]
-    g1 = [r1] + [x_shift(r1, s) for s in range(1, 4)]
-    g23 = [r23] + [x_shift(r23, s) for s in range(1, 4)]
-
-    parts = [received] + [x_shift(received, s) for s in range(1, 4)]
-    parts = jnp.stack(parts)
-    column = jnp.concatenate(
-        [lax.dynamic_index_in_dim(parts, lax.rem(me + 4 - i, 4), 0, keepdims=False) for i in range(4)], axis=0
-    )
+        return jnp.concatenate(diag_part(s) + offs, axis=0)
+
+    def head_part(s):
+        return jnp.concatenate(diag_part(s) + [child_part(s)], axis=0)
+
+    rest = rest_part(0)
+    rest_got = [x_from0(rest_part(s), s, range(1, 4)) for s in range(1, 4)]
+    head = own_or(me == 0, head_part(0), *[x_from0(head_part(s), s, range(3)) for s in range(1, 4)])
+    head_z = own_or(col < 4, head, *[z_from0(head, s) for s in range(1, 4)])
+    head_y = by_source(head_z, y_shift, y, range(3))
+    g0 = jnp.concatenate([head_y[0]] + [h[DIAG:] for h in head_y[1:]], axis=0)
+    g0 = [g0] + [x_shift(g0, s) for s in range(1, 4)]
+    rest = own_or(me == 0, rest, *after(rest_got, head_z))
+    rest = own_or(col < 4, rest, *[z_from0(rest, s) for s in range(1, 4)])
+    rest = after(rest, head_y[0])
+    rest_y = by_source(rest, y_shift, y, range(1, 4))
+    g1 = rest_y[0][: DIAG + PIECE]
+    g1 = [g1] + [x_shift(g1, s) for s in range(1, 4)]
+    g23 = jnp.concatenate([rest_y[1][: DIAG + 2 * PIECE], rest_y[2]], axis=0)
+    g23 = [g23] + [x_shift(g23, s) for s in range(1, 4)]
+
+    column = jnp.concatenate(by_source(after(received, head_z), x_shift, me, range(4)), axis=0)
     first = jnp.where(me == 3, 4, 0)
     chosen = lax.dynamic_slice_in_dim(column, first * BLK, 12 * BLK, 0)
-    thick = []
-    for j in range(THICK):
-        pairs = [(SOURCES[c][j], c) for c in SOURCES if j < len(SOURCES[c])]
-        thick.append(lax.ppermute(column, "col", pairs))
-
     panel_wide = jnp.concatenate([high, chosen], axis=1)
-    wide = jnp.where(col < 4, panel_wide[:PANEL], jnp.zeros((), BF16))
-    for s in range(1, 4):
-        wide = wide + z_from0(panel_wide[s * PANEL : (s + 1) * PANEL], s)
+    wide = own_or(
+        col < 4, panel_wide[:PANEL], *[z_from0(panel_wide[s * PANEL : (s + 1) * PANEL], s) for s in range(1, 4)]
+    )
     wide = lax.all_gather(wide, "col")
-    a12 = high
-    got = jnp.zeros((), BF16)
-    for s in range(1, 4):
-        got = got + x_from0(high, s, range(4, N_COL))
-    a12 = got
+    a12 = after(high, g0[0], g0[1])
+    got = [x_from0(a12, s, range(4, N_COL)) for s in range(1, 4)]
+    a12 = got[0] + got[1] + got[2]
 
     ids = jnp.full((N_COL, THICK), -1, jnp.int32)
     for c in SOURCES:
@@ -492,15 +507,22 @@
 
     ups, invs, lows, mines = [], [], [], []
     flat_invs = []
+    thick = None
     for k in range(PANELS):
         pieces = [g0, g1, g23, g23][k]
-        base = 4 * PIECE if k == 3 else 0
+        base = DIAG + 2 * PIECE if k == 3 else 0
         ih, il, up, low, mine_out = panel_call(k, base, info, index_map, pieces, g0, ups, flat_invs)
         flat_invs += [ih, il]
         ups.append(up)
         invs.append(ih)
         lows.append(low)
         mines.append(mine_out)
+        if k == 0:
+            late = after(column, ih)
+            thick = []
+            for j in range(THICK):
+                pairs = [(SOURCES[c][j], c) for c in SOURCES if j < len(SOURCES[c])]
+                thick.append(lax.ppermute(late, "col", pairs))
     out = tail_call(info, index_map, front, a12, wide, thick, g0, ups[1:], invs, lows, mines[1:])
     return out[None]
 

time: 286 us -> 291 us (1.017)
  the two profiles are of different devices: /device:TPU:46 before, /device:TPU:101 now
where the time goes in v2:
time: 291 us; the launch traced here: 287 us
  Pallas kernels  101 us (35%)
  waiting for transfers between devices  85.2 us (29%)
  starting transfers between devices  64.8 us (22%)
  between operations  14.5 us (5%)
  other arithmetic  14.1 us (5%)
  local copies, waits for them, and re-layouts  7.58 us (3%)
    pallas_call x4, Pallas kernels, panel_call(): pl.pallas_call(functools.partial(panel_kernel, k, base), out_shape=[jax.S...  73.5 us
    ppermute x5, waiting for transfers between devices, per_device(): thick.append(lax.ppermute(late, 'col', pairs))  39.9 us
    ppermute x12, starting transfers between devices, x_shift(): return lax.ppermute(value, 'row', [(i, (i + s) % 4) for i in range(4)])  29.2 us
    pallas_call x1, Pallas kernels, tail_call(): pl.pallas_call(tail_kernel, out_shape=jax.ShapeDtypeStruct((LEAD, PANEL),...  27.6 us
    ppermute x9, waiting for transfers between devices, z_from0(): return lax.ppermute(value, 'col', [(b, 4 * s + b) for b in range(4)])  25.2 us
    ppermute x12, waiting for transfers between devices, x_shift(): return lax.ppermute(value, 'row', [(i, (i + s) % 4) for i in range(4)])  17.3 us
    ppermute x6, starting transfers between devices, y_shift(): lax.ppermute(value, 'col', [(4 * z + b, 4 * z + (b + s) % 4) for z in ran...  10.6 us
    ppermute x5, starting transfers between devices, per_device(): thick.append(lax.ppermute(late, 'col', pairs))  8.76 us
  transfers between devices with their start and end apart: 43, of which 14 were waited for; matrix products, arithmetic and copies ran while one was open for 5% of the time, Pallas kernels for 26%

profile of v2, /device:TPU:101, one launch (start us, length us, event | category | flops | bytes accessed | tf_op | source)
XLA Modules:
  0.0 287.3 jit_solution(553966669552348041)
XLA Ops:
  7.2 1.1 dynamic-slice_bitcast_fusion
  8.4 0.9 dynamic-slice_bitcast_fusion.12
  12.5 0.8 collective-permute-start.1
  15.3 1.3 collective-permute-start.2
  16.6 1.0 fusion.9
  17.6 1.3 collective-permute-start.6
  20.3 8.1 %collective-permute-done.6 = bf16[160,384]{1,0:T(8,128)(2,1)S(1)} collective-permute-done((bf16[160,384]{1,0:T(8,128)(2,1)S(1)}, bf16[160,384]{1,0:T(8,128)(2,1)S(1)}, u32[]{:S(2)}, u32[]{:S(2)}) %collective-permute-start.6) | collective-permute-done | bytes 122912 | tf_op jit(solution)/shard_map/ppermute | solution.py:426
  29.1 0.8 collective-permute-start.14
  30.0 1.1 bitcast_convert_fusion
  31.1 1.2 collective-permute-done.16
  32.3 1.7 collective-permute-done.15
  34.0 3.3 %collective-permute-done.14 = bf16[512,128]{1,0:T(8,128)(2,1)} collective-permute-done((bf16[512,128]{1,0:T(8,128)(2,1)S(1)}, bf16[512,128]{1,0:T(8,128)(2,1)}, u32[]{:S(2)}, u32[]{:S(2)}) %collective-permute-start.14) | collective-permute-done | bytes 131104 | tf_op jit(solution)/shard_map/ppermute | solution.py:429
  37.3 1.0 pad_maximum_fusion.2
  38.5 1.2 fusion.6
  39.7 0.7 collective-permute-start.17
  40.4 1.3 collective-permute-start.19
  41.7 0.8 collective-permute-start.18
  42.6 13.7 %collective-permute-done.19 = bf16[384,512]{1,0:T(8,128)(2,1)S(1)} collective-permute-done((bf16[384,512]{1,0:T(8,128)(2,1)S(1)}, bf16[384,512]{1,0:T(8,128)(2,1)S(1)}, u32[]{:S(2)}, u32[]{:S(2)}) %collective-permute-start.19) | collective-permute-done | bytes 393248 | tf_op jit(solution)/shard_map/ppermute | solution.py:426
  56.3 1.9 fusion.5
  58.3 1.0 slice_dynamic-update-slice_fusion.11
  59.4 1.0 slice_dynamic-update-slice_fusion.10
  60.4 1.0 slice_dynamic-update-slice_fusion.9
  61.5 0.7 collective-permute-start.29
  62.2 0.7 collective-permute-start.28
  62.8 0.7 collective-permute-start.27
  63.6 0.7 maximum_bitcast_fusion
  65.5 2.6 collective-permute-start.8
  68.1 0.7 collective-permute-start.7
  68.9 1.3 collective-permute-start.32
  70.2 0.7 collective-permute-start.31
  70.9 0.7 collective-permute-start.30
  71.6 2.8 collective-permute-done.7
  74.6 0.7 bitcast_select_fusion.1
  75.4 1.5 collective-permute-start.21
  76.9 2.0 collective-permute-done.10.refs_1_.refs_5_.refs_6_
  78.9 2.8 collective-permute-start.20
  81.7 3.4 %collective-permute-done.32 = bf16[416,384]{1,0:T(8,128)(2,1)S(1)} collective-permute-done((bf16[416,384]{1,0:T(8,128)(2,1)S(1)}, bf16[416,384]{1,0:T(8,128)(2,1)S(1)}, u32[]{:S(2)}, u32[]{:S(2)}) %collective-permute-start.32) | collective-permute-done | bytes 319520 | tf_op jit(solution)/shard_map/ppermute | solution.py:426
  85.1 0.7 collective-permute-start.13
  85.8 1.3 collective-permute-start.12
  87.2 4.2 %collective-permute-start.35 = (bf16[416,384]{1,0:T(8,128)(2,1)S(1)}, bf16[416,384]{1,0:T(8,128)(2,1)S(1)}, u32[]{:S(2)}, u32[]{:S(2)}) collective-permute-start(bf16[416,384]{1,0:T(8,128)(2,1)S(1)} %add_add_fusion.1), channel_id=1, source_target_pairs={{0,3},{1,0},{2,1},{3,2},{4,7},{5,4},{6,5},{7,6},{8,11},{9,8},{10,9... | collective-permute-start | bytes 958472 | tf_op jit(solution)/shard_map/ppermute | solution.py:432
  91.5 1.9 collective-permute-start.34
  94.0 14.0 %panel0.1 = (bf16[384,384]{1,0:T(8,128)(2,1)S(1)}, bf16[384,384]{1,0:T(8,128)(2,1)S(1)}, bf16[16,384]{1,0:T(8,128)(2,1)S(1)}, f32[384,384]{1,0:T(8,128)S(1)}, f32[384,384]{1,0:T(8,128)}) custom-call(s32[16]{0:T(128)S(1)} %concatenate.125.info, s32[16]{0:T(128)S(1)} %bitcast.61, bf16[224,384]{1,0:T(8,128)(2,1)S(1)} %pad_maximum_fusion.6.refs_0_.refs_4_.refs_5_, ...), custom_call_target="tpu_custom_call" | custom-call | flops 10000000000 | bytes 1000000 | tf_op jit(solution)/shard_map/panel0/pallas_call | solution.py:210
  108.8 15.3 %collective-permute-start.38 = (bf16[224,384]{1,0:T(8,128)(2,1)S(1)}, bf16[224,384]{1,0:T(8,128)(2,1)S(1)}, u32[]{:S(2)}, u32[]{:S(2)}) collective-permute-start(bf16[224,384]{1,0:T(8,128)(2,1)S(1)} %dynamic-slice_bitcast_fusion.3.refs_0_), channel_id=1, source_target_pairs={{0,48},{16,0},{32,16},{48,32},{1,49},{17,1},{33,17},{49,33},{2,50}... | collective-permute-start | bytes 516104 | tf_op jit(solution)/shard_map/ppermute | solution.py:429
  124.1 1.8 collective-permute-start.37
  125.9 2.3 collective-permute-start.36
  128.7 1.5 collective-permute-done.37.refs_2_
  130.2 1.5 collective-permute-start.40
  132.1 2.0 collective-permute-start.39
  134.1 14.5 %panel1.1 = (bf16[384,384]{1,0:T(8,128)(2,1)S(1)}, bf16[384,384]{1,0:T(8,128)(2,1)S(1)}, bf16[384,384]{1,0:T(8,128)(2,1)S(1)}, f32[384,384]{1,0:T(8,128)S(1)}, f32[384,384]{1,0:T(8,128)S(1)}) custom-call(s32[16]{0:T(128)S(1)} %concatenate.125.info, s32[16]{0:T(128)S(1)} %bitcast.62, bf16[224,384]{1,0:T(8,128)(2,1)S(1)} %dynamic-slice_bitcast_fusion.3.refs_0_, ...), custom_call_target="tpu_custom_call" | custom-call | flops 10000000000 | bytes 1000000 | tf_op jit(solution)/shard_map/panel1/pallas_call | solution.py:210
  148.6 0.7 collective-permute-start.11
  149.4 1.3 collective-permute-start.26
  150.7 7.2 %collective-permute-done.39.refs_1_ = bf16[736,384]{1,0:T(8,128)(2,1)S(1)} collective-permute-done((bf16[736,384]{1,0:T(8,128)(2,1)S(1)}, bf16[736,384]{1,0:T(8,128)(2,1)S(1)}, u32[]{:S(2)}, u32[]{:S(2)}) %collective-permute-start.39) | collective-permute-done | bytes 565280 | tf_op jit(solution)/shard_map/ppermute | solution.py:429
  157.9 1.3 collective-permute-start.25
  159.2 15.8 %panel2.1 = (bf16[384,384]{1,0:T(8,128)(2,1)S(1)}, bf16[384,384]{1,0:T(8,128)(2,1)S(1)}, bf16[768,384]{1,0:T(8,128)(2,1)S(1)}, f32[384,384]{1,0:T(8,128)S(1)}, f32[384,384]{1,0:T(8,128)S(1)}) custom-call(s32[16]{0:T(128)S(1)} %concatenate.125.info, s32[16]{0:T(128)S(1)} %bitcast.63, bf16[736,384]{1,0:T(8,128)(2,1)S(1)} %pad_maximum_fusion.1.refs_0_, ...), custom_call_target="tpu_custom_call" | custom-call | flops 10000000000 | bytes 1000000 | tf_op jit(solution)/shard_map/panel2/pallas_call | solution.py:210
  175.1 29.1 %panel3.1 = (bf16[384,384]{1,0:T(8,128)(2,1)S(1)}, bf16[384,384]{1,0:T(8,128)(2,1)}, bf16[1152,384]{1,0:T(8,128)(2,1)S(1)}, f32[384,384]{1,0:T(8,128)S(1)}, f32[384,384]{1,0:T(8,128)S(1)}) custom-call(s32[16]{0:T(128)S(1)} %concatenate.125.info, s32[16]{0:T(128)S(1)} %bitcast.64, bf16[736,384]{1,0:T(8,128)(2,1)S(1)} %pad_maximum_fusion.1.refs_0_, ...), custom_call_target="tpu_custom_call" | custom-call | flops 10000000000 | bytes 1000000 | tf_op jit(solution)/shard_map/panel3/pallas_call | solution.py:210
  204.4 3.6 %collective-permute-start.24 = (bf16[2048,128]{1,0:T(8,128)(2,1)S(1)}, bf16[2048,128]{1,0:T(8,128)(2,1)S(1)}, u32[]{:S(2)}, u32[]{:S(2)}) collective-permute-start(bf16[2048,128]{1,0:T(8,128)(2,1)S(1)} %pad_maximum_fusion.3), channel_id=1, source_target_pairs={{5,11},{6,12},{9,13},{12,14},{15,15},{21,27},{22,28},{25,29},{28,3... | collective-permute-start | bytes 1572872 | tf_op jit(solution)/shard_map/ppermute | solution.py:525
  208.0 1.3 collective-permute-start.23
  209.3 1.3 collective-permute-start.22
  210.6 1.3 add_add_fusion.a12
  211.9 14.5 %collective-permute-done.24.refs_2_ = bf16[2048,128]{1,0:T(8,128)(2,1)S(1)} collective-permute-done((bf16[2048,128]{1,0:T(8,128)(2,1)S(1)}, bf16[2048,128]{1,0:T(8,128)(2,1)S(1)}, u32[]{:S(2)}, u32[]{:S(2)}) %collective-permute-start.24) | collective-permute-done | bytes 524320 | tf_op jit(solution)/shard_map/ppermute | solution.py:525
  226.4 15.5 %collective-permute-done.23.refs_1_ = bf16[2048,128]{1,0:T(8,128)(2,1)S(1)} collective-permute-done((bf16[2048,128]{1,0:T(8,128)(2,1)S(1)}, bf16[2048,128]{1,0:T(8,128)(2,1)S(1)}, u32[]{:S(2)}, u32[]{:S(2)}) %collective-permute-start.23) | collective-permute-done | bytes 524320 | tf_op jit(solution)/shard_map/ppermute | solution.py:525
  242.0 9.9 %collective-permute-done.22.refs_0_ = bf16[2048,128]{1,0:T(8,128)(2,1)S(1)} collective-permute-done((bf16[2048,128]{1,0:T(8,128)(2,1)S(1)}, bf16[2048,128]{1,0:T(8,128)(2,1)S(1)}, u32[]{:S(2)}, u32[]{:S(2)}) %collective-permute-start.22) | collective-permute-done | bytes 524320 | tf_op jit(solution)/shard_map/ppermute | solution.py:525
  251.9 0.8 copy-done.28
  252.7 27.6 %tail.1 = f32[1536,384]{1,0:T(8,128)} custom-call(s32[16]{0:T(128)} %copy-done.2, s32[16]{0:T(128)} %bitcast.59, f32[1536,384]{1,0:T(8,128)} %bitcast.65, bf16[1536,384]{1,0:T(8,128)(2,1)} %add_add_fusion.a12, bf16[16,384,512]{2,1,0:T(8,128)(2,1)} %bitcast.77, bf16[2048,128]{1,0:T(8,128)(2,1)} %copy-done.28, bf16[2048,128]{1,0:T(8,128)(2,1)} %copy-done.27, ...), custom_call_target="tpu_custom_call" | custom-call | flops 7000000000 | bytes 20000000 | tf_op jit(solution)/shard_map/tail/pallas_call | solution.py:395
  (132 shorter events, 12.2 us)
Async XLA Ops:
  6.5 245.3 %all-gather.3.cloned.1.call-start = ((), (), s32[]{:S(2)}) async-start(), calls=%async_computation | async-start | bytes 6684672 | tf_op jit(solution)/shard_map/all_gather | solution.py:493
  6.5 5.9 %collective-permute-start = (bf16[512,128]{1,0:T(8,128)(2,1)}, bf16[512,128]{1,0:T(8,128)(2,1)S(1)}, u32[]{:S(2)}, u32[]{:S(2)}) collective-permute-start(bf16[512,128]{1,0:T(8,128)(2,1)} %bitcast.78), channel_id=1, source_target_pairs={{0,64},{64,0},{1,65},{65,1},{2,66},{66,2},{3,67},{67,3},{4,68},{68... | collective-permute-start | bytes 393224 | tf_op jit(solution)/shard_map/ppermute | solution.py:447
  12.4 17.5 %copy-start.20 = (f32[1,1536,384]{2,1,0:T(8,128)S(1)}, f32[1,1536,384]{2,1,0:T(8,128)}, u32[]{:S(2)}) copy-start(f32[1,1536,384]{2,1,0:T(8,128)} %param.45) | copy-start | bytes 7077892
  12.5 4.2 %collective-permute-start.1 = (bf16[160,384]{1,0:T(8,128)(2,1)S(1)}, bf16[160,384]{1,0:T(8,128)(2,1)S(1)}, u32[]{:S(2)}, u32[]{:S(2)}) collective-permute-start(bf16[160,384]{1,0:T(8,128)(2,1)S(1)} %maximum_maximum_fusion), channel_id=1, source_target_pairs={{0,16},{1,17},{2,18},{64,80},{65,81},{66,82}} | collective-permute-start | bytes 368648 | tf_op jit(solution)/shard_map/ppermute | solution.py:423
  13.9 2.7 collective-permute-start.3
  15.3 1.4 collective-permute-start.2
  17.6 10.7 %collective-permute-start.6 = (bf16[160,384]{1,0:T(8,128)(2,1)S(1)}, bf16[160,384]{1,0:T(8,128)(2,1)S(1)}, u32[]{:S(2)}, u32[]{:S(2)}) collective-permute-start(bf16[160,384]{1,0:T(8,128)(2,1)S(1)} %fusion.9), channel_id=1, source_target_pairs={{0,12},{1,13},{2,14},{3,15},{16,28},{17,29},{18,30},{19,31},{32,44... | collective-permute-start | bytes 368648 | tf_op jit(solution)/shard_map/ppermute | solution.py:426
  18.9 9.4 %collective-permute-start.5 = (bf16[160,384]{1,0:T(8,128)(2,1)S(1)}, bf16[160,384]{1,0:T(8,128)(2,1)S(1)}, u32[]{:S(2)}, u32[]{:S(2)}) collective-permute-start(bf16[160,384]{1,0:T(8,128)(2,1)S(1)} %fusion.9), channel_id=1, source_target_pairs={{0,8},{1,9},{2,10},{3,11},{16,24},{17,25},{18,26},{19,27},{32,40},... | collective-permute-start | bytes 368648 | tf_op jit(solution)/shard_map/ppermute | solution.py:426
  19.6 8.8 %collective-permute-start.4 = (bf16[160,384]{1,0:T(8,128)(2,1)S(1)}, bf16[160,384]{1,0:T(8,128)(2,1)S(1)}, u32[]{:S(2)}, u32[]{:S(2)}) collective-permute-start(bf16[160,384]{1,0:T(8,128)(2,1)S(1)} %fusion.9), channel_id=1, source_target_pairs={{0,4},{1,5},{2,6},{3,7},{16,20},{17,21},{18,22},{19,23},{32,36},{3... | collective-permute-start | bytes 368648 | tf_op jit(solution)/shard_map/ppermute | solution.py:426
  28.4 3.9 %collective-permute-start.16 = (bf16[512,128]{1,0:T(8,128)(2,1)S(1)}, bf16[512,128]{1,0:T(8,128)(2,1)S(1)}, u32[]{:S(2)}, u32[]{:S(2)}) collective-permute-start(bf16[512,128]{1,0:T(8,128)(2,1)S(1)} %collective-permute-done), channel_id=1, source_target_pairs={{0,48},{16,0},{32,16},{48,32},{1,49},{17,1},{33,17},{49,33},{2,50}... | collective-permute-start | bytes 393224 | tf_op jit(solution)/shard_map/ppermute | solution.py:429
  28.5 5.5 %collective-permute-start.15 = (bf16[512,128]{1,0:T(8,128)(2,1)S(1)}, bf16[512,128]{1,0:T(8,128)(2,1)S(1)}, u32[]{:S(2)}, u32[]{:S(2)}) collective-permute-start(bf16[512,128]{1,0:T(8,128)(2,1)S(1)} %collective-permute-done), channel_id=1, source_target_pairs={{0,32},{16,48},{32,0},{48,16},{1,33},{17,49},{33,1},{49,17},{2,34}... | collective-permute-start | bytes 393224 | tf_op jit(solution)/shard_map/ppermute | solution.py:429
  29.1 8.2 %collective-permute-start.14 = (bf16[512,128]{1,0:T(8,128)(2,1)S(1)}, bf16[512,128]{1,0:T(8,128)(2,1)}, u32[]{:S(2)}, u32[]{:S(2)}) collective-permute-start(bf16[512,128]{1,0:T(8,128)(2,1)S(1)} %collective-permute-done), channel_id=1, source_target_pairs={{0,16},{16,32},{32,48},{48,0},{1,17},{17,33},{33,49},{49,1},{2,18}... | collective-permute-start | bytes 393224 | tf_op jit(solution)/shard_map/ppermute | solution.py:429
  39.7 2.9 collective-permute-start.17
  40.4 15.9 %collective-permute-start.19 = (bf16[384,512]{1,0:T(8,128)(2,1)S(1)}, bf16[384,512]{1,0:T(8,128)(2,1)S(1)}, u32[]{:S(2)}, u32[]{:S(2)}) collective-permute-start(bf16[384,512]{1,0:T(8,128)(2,1)S(1)} %get-tuple-element.340), channel_id=1, source_target_pairs={{0,12},{1,13},{2,14},{3,15},{16,28},{17,29},{18,30},{19,31},{32,44... | collective-permute-start | bytes 1179656 | tf_op jit(solution)/shard_map/ppermute | solution.py:426
  41.7 16.6 %copy-start.21 = (bf16[416,384]{1,0:T(8,128)(2,1)S(1)}, bf16[416,384]{1,0:T(8,128)(2,1)}, u32[]{:S(2)}) copy-start(bf16[416,384]{1,0:T(8,128)(2,1)} %get-tuple-element.331) | copy-start | bytes 958468
  41.7 16.6 %copy-start.22 = (bf16[416,384]{1,0:T(8,128)(2,1)S(1)}, bf16[416,384]{1,0:T(8,128)(2,1)}, u32[]{:S(2)}) copy-start(bf16[416,384]{1,0:T(8,128)(2,1)} %get-tuple-element.329) | copy-start | bytes 958468
  41.7 16.6 %copy-start.23 = (bf16[416,384]{1,0:T(8,128)(2,1)S(1)}, bf16[416,384]{1,0:T(8,128)(2,1)}, u32[]{:S(2)}) copy-start(bf16[416,384]{1,0:T(8,128)(2,1)} %get-tuple-element.333) | copy-start | bytes 958468
  41.7 14.6 %collective-permute-start.18 = (bf16[384,512]{1,0:T(8,128)(2,1)S(1)}, bf16[384,512]{1,0:T(8,128)(2,1)S(1)}, u32[]{:S(2)}, u32[]{:S(2)}) collective-permute-start(bf16[384,512]{1,0:T(8,128)(2,1)S(1)} %get-tuple-element.341), channel_id=1, source_target_pairs={{0,8},{1,9},{2,10},{3,11},{16,24},{17,25},{18,26},{19,27},{32,40},... | collective-permute-start | bytes 1179656 | tf_op jit(solution)/shard_map/ppermute | solution.py:426
  61.5 6.6 %collective-permute-start.29 = (bf16[416,384]{1,0:T(8,128)(2,1)S(1)}, bf16[416,384]{1,0:T(8,128)(2,1)S(1)}, u32[]{:S(2)}, u32[]{:S(2)}) collective-permute-start(bf16[416,384]{1,0:T(8,128)(2,1)S(1)} %get-tuple-element.343), channel_id=1, source_target_pairs={{1,49},{2,50},{3,51},{65,113},{66,114},{67,115}} | collective-permute-start | bytes 958472 | tf_op jit(solution)/shard_map/ppermute | solution.py:423
  62.2 6.6 %collective-permute-start.28 = (bf16[416,384]{1,0:T(8,128)(2,1)S(1)}, bf16[416,384]{1,0:T(8,128)(2,1)S(1)}, u32[]{:S(2)}, u32[]{:S(2)}) collective-permute-start(bf16[416,384]{1,0:T(8,128)(2,1)S(1)} %get-tuple-element.344), channel_id=1, source_target_pairs={{1,33},{2,34},{3,35},{65,97},{66,98},{67,99}} | collective-permute-start | bytes 958472 | tf_op jit(solution)/shard_map/ppermute | solution.py:423
  62.8 5.9 %collective-permute-start.27 = (bf16[416,384]{1,0:T(8,128)(2,1)S(1)}, bf16[416,384]{1,0:T(8,128)(2,1)S(1)}, u32[]{:S(2)}, u32[]{:S(2)}) collective-permute-start(bf16[416,384]{1,0:T(8,128)(2,1)S(1)} %get-tuple-element.345), channel_id=1, source_target_pairs={{1,17},{2,18},{3,19},{65,81},{66,82},{67,83}} | collective-permute-start | bytes 958472 | tf_op jit(solution)/shard_map/ppermute | solution.py:423
  64.9 5.9 %collective-permute-start.9 = (bf16[160,384]{1,0:T(8,128)(2,1)S(1)}, bf16[160,384]{1,0:T(8,128)(2,1)S(1)}, u32[]{:S(2)}, u32[]{:S(2)}) collective-permute-start(bf16[160,384]{1,0:T(8,128)(2,1)S(1)} %add_add_fusion.3), channel_id=1, source_target_pairs={{0,3},{1,0},{2,1},{3,2},{4,7},{5,4},{6,5},{7,6},{8,11},{9,8},{10,9... | collective-permute-start | bytes 368648 | tf_op jit(solution)/shard_map/ppermute | solution.py:432
  65.5 6.1 %collective-permute-start.8 = (bf16[160,384]{1,0:T(8,128)(2,1)S(1)}, bf16[160,384]{1,0:T(8,128)(2,1)S(1)}, u32[]{:S(2)}, u32[]{:S(2)}) collective-permute-start(bf16[160,384]{1,0:T(8,128)(2,1)S(1)} %add_add_fusion.3), channel_id=1, source_target_pairs={{0,2},{1,3},{2,0},{3,1},{4,6},{5,7},{6,4},{7,5},{8,10},{9,11},{10,... | collective-permute-start | bytes 368648 | tf_op jit(solution)/shard_map/ppermute | solution.py:432
  68.1 6.3 %collective-permute-start.7 = (bf16[160,384]{1,0:T(8,128)(2,1)S(1)}, bf16[160,384]{1,0:T(8,128)(2,1)S(1)}, u32[]{:S(2)}, u32[]{:S(2)}) collective-permute-start(bf16[160,384]{1,0:T(8,128)(2,1)S(1)} %add_add_fusion.3), channel_id=1, source_target_pairs={{0,1},{1,2},{2,3},{3,0},{4,5},{5,6},{6,7},{7,4},{8,9},{9,10},{10,1... | collective-permute-start | bytes 368648 | tf_op jit(solution)/shard_map/ppermute | solution.py:432
  68.9 16.2 %collective-permute-start.32 = (bf16[416,384]{1,0:T(8,128)(2,1)S(1)}, bf16[416,384]{1,0:T(8,128)(2,1)S(1)}, u32[]{:S(2)}, u32[]{:S(2)}) collective-permute-start(bf16[416,384]{1,0:T(8,128)(2,1)S(1)} %add_add_fusion.2), channel_id=1, source_target_pairs={{0,12},{1,13},{2,14},{3,15},{16,28},{17,29},{18,30},{19,31},{32,44... | collective-permute-start | bytes 958472 | tf_op jit(solution)/shard_map/ppermute | solution.py:426
  70.2 15.6 %collective-permute-start.31 = (bf16[416,384]{1,0:T(8,128)(2,1)S(1)}, bf16[416,384]{1,0:T(8,128)(2,1)S(1)}, u32[]{:S(2)}, u32[]{:S(2)}) collective-permute-start(bf16[416,384]{1,0:T(8,128)(2,1)S(1)} %add_add_fusion.2), channel_id=1, source_target_pairs={{0,8},{1,9},{2,10},{3,11},{16,24},{17,25},{18,26},{19,27},{32,40},... | collective-permute-start | bytes 958472 | tf_op jit(solution)/shard_map/ppermute | solution.py:426
  70.9 16.2 %collective-permute-start.30 = (bf16[416,384]{1,0:T(8,128)(2,1)S(1)}, bf16[416,384]{1,0:T(8,128)(2,1)S(1)}, u32[]{:S(2)}, u32[]{:S(2)}) collective-permute-start(bf16[416,384]{1,0:T(8,128)(2,1)S(1)} %add_add_fusion.2), channel_id=1, source_target_pairs={{0,4},{1,5},{2,6},{3,7},{16,20},{17,21},{18,22},{19,23},{32,36},{3... | collective-permute-start | bytes 958472 | tf_op jit(solution)/shard_map/ppermute | solution.py:426
  74.5 100.5 %copy-start.1 = (bf16[224,384]{1,0:T(8,128)(2,1)}, bf16[224,384]{1,0:T(8,128)(2,1)S(1)}, u32[]{:S(2)}) copy-start(bf16[224,384]{1,0:T(8,128)(2,1)S(1)} %pad_maximum_fusion.6.refs_0_.refs_4_.refs_5_) | copy-start | bytes 516100
  74.5 4.3 %collective-permute-start.10 = (bf16[224,384]{1,0:T(8,128)(2,1)S(1)}, bf16[224,384]{1,0:T(8,128)(2,1)S(1)}, u32[]{:S(2)}, u32[]{:S(2)}) collective-permute-start(bf16[224,384]{1,0:T(8,128)(2,1)S(1)} %pad_maximum_fusion.6.refs_0_.refs_4_.refs_5_), channel_id=1, source_target_pairs={{0,16},{16,32},{32,48},{48,0},{1,17},{17,33},{33,49},{49,1},{2,18}... | collective-permute-start | bytes 516104 | tf_op jit(solution)/shard_map/ppermute | solution.py:429
  75.4 99.7 %copy-start.2 = (s32[16]{0:T(128)}, s32[16]{0:T(128)S(1)}, u32[]{:S(2)}) copy-start(s32[16]{0:T(128)S(1)} %concatenate.125.info) | copy-start | bytes 196
  75.4 16.1 %collective-permute-start.21 = (bf16[224,384]{1,0:T(8,128)(2,1)S(1)}, bf16[224,384]{1,0:T(8,128)(2,1)S(1)}, u32[]{:S(2)}, u32[]{:S(2)}) collective-permute-start(bf16[224,384]{1,0:T(8,128)(2,1)S(1)} %pad_maximum_fusion.6.refs_0_.refs_4_.refs_5_), channel_id=1, source_target_pairs={{0,48},{16,0},{32,16},{48,32},{1,49},{17,1},{33,17},{49,33},{2,50}... | collective-permute-start | bytes 516104 | tf_op jit(solution)/shard_map/ppermute | solution.py:429
  78.9 96.2 %copy-start.3 = (bf16[224,384]{1,0:T(8,128)(2,1)}, bf16[224,384]{1,0:T(8,128)(2,1)S(1)}, u32[]{:S(2)}) copy-start(bf16[224,384]{1,0:T(8,128)(2,1)S(1)} %collective-permute-done.10.refs_1_.refs_5_.refs_6_) | copy-start | bytes 516100
  78.9 14.5 %collective-permute-start.20 = (bf16[224,384]{1,0:T(8,128)(2,1)S(1)}, bf16[224,384]{1,0:T(8,128)(2,1)S(1)}, u32[]{:S(2)}, u32[]{:S(2)}) collective-permute-start(bf16[224,384]{1,0:T(8,128)(2,1)S(1)} %pad_maximum_fusion.6.refs_0_.refs_4_.refs_5_), channel_id=1, source_target_pairs={{0,32},{16,48},{32,0},{48,16},{1,33},{17,49},{33,1},{49,17},{2,34}... | collective-permute-start | bytes 516104 | tf_op jit(solution)/shard_map/ppermute | solution.py:429
  85.1 119.3 %collective-permute-start.13 = (bf16[1536,384]{1,0:T(8,128)(2,1)}, bf16[1536,384]{1,0:T(8,128)(2,1)S(1)}, u32[]{:S(2)}, u32[]{:S(2)}) collective-permute-start(bf16[1536,384]{1,0:T(8,128)(2,1)} %bitcast_convert_fusion), channel_id=1, source_target_pairs={{4,52},{5,53},{6,54},{7,55},{8,56},{9,57},{10,58},{11,59},{12,60},... | collective-permute-start | bytes 3538952 | tf_op jit(solution)/shard_map/ppermute | solution.py:423
  85.8 122.2 %collective-permute-start.12 = (bf16[1536,384]{1,0:T(8,128)(2,1)}, bf16[1536,384]{1,0:T(8,128)(2,1)S(1)}, u32[]{:S(2)}, u32[]{:S(2)}) collective-permute-start(bf16[1536,384]{1,0:T(8,128)(2,1)} %bitcast_convert_fusion), channel_id=1, source_target_pairs={{4,36},{5,37},{6,38},{7,39},{8,40},{9,41},{10,42},{11,43},{12,44},... | collective-permute-start | bytes 3538952 | tf_op jit(solution)/shard_map/ppermute | solution.py:423
  87.2 20.8 %collective-permute-start.35 = (bf16[416,384]{1,0:T(8,128)(2,1)S(1)}, bf16[416,384]{1,0:T(8,128)(2,1)S(1)}, u32[]{:S(2)}, u32[]{:S(2)}) collective-permute-start(bf16[416,384]{1,0:T(8,128)(2,1)S(1)} %add_add_fusion.1), channel_id=1, source_target_pairs={{0,3},{1,0},{2,1},{3,2},{4,7},{5,4},{6,5},{7,6},{8,11},{9,8},{10,9... | collective-permute-start | bytes 958472 | tf_op jit(solution)/shard_map/ppermute | solution.py:432
  91.5 83.6 %copy-start.4 = (bf16[224,384]{1,0:T(8,128)(2,1)}, bf16[224,384]{1,0:T(8,128)(2,1)S(1)}, u32[]{:S(2)}) copy-start(bf16[224,384]{1,0:T(8,128)(2,1)S(1)} %collective-permute-done.21.refs_3_.refs_7_.refs_8_) | copy-start | bytes 516100
  91.5 16.5 %collective-permute-start.34 = (bf16[416,384]{1,0:T(8,128)(2,1)S(1)}, bf16[416,384]{1,0:T(8,128)(2,1)S(1)}, u32[]{:S(2)}, u32[]{:S(2)}) collective-permute-start(bf16[416,384]{1,0:T(8,128)(2,1)S(1)} %add_add_fusion.1), channel_id=1, source_target_pairs={{0,2},{1,3},{2,0},{3,1},{4,6},{5,7},{6,4},{7,5},{8,10},{9,11},{10,... | collective-permute-start | bytes 958472 | tf_op jit(solution)/shard_map/ppermute | solution.py:432
  93.4 81.7 %copy-start.5 = (bf16[224,384]{1,0:T(8,128)(2,1)}, bf16[224,384]{1,0:T(8,128)(2,1)S(1)}, u32[]{:S(2)}) copy-start(bf16[224,384]{1,0:T(8,128)(2,1)S(1)} %collective-permute-done.20.refs_2_.refs_6_.refs_7_) | copy-start | bytes 516100
  93.4 14.6 %collective-permute-start.33 = (bf16[416,384]{1,0:T(8,128)(2,1)S(1)}, bf16[416,384]{1,0:T(8,128)(2,1)S(1)}, u32[]{:S(2)}, u32[]{:S(2)}) collective-permute-start(bf16[416,384]{1,0:T(8,128)(2,1)S(1)} %add_add_fusion.1), channel_id=1, source_target_pairs={{0,1},{1,2},{2,3},{3,0},{4,5},{5,6},{6,7},{7,4},{8,9},{9,10},{10,1... | collective-permute-start | bytes 958472 | tf_op jit(solution)/shard_map/ppermute | solution.py:432
  108.0 67.1 %copy-start.15 = (bf16[384,384]{1,0:T(8,128)(2,1)}, bf16[384,384]{1,0:T(8,128)(2,1)S(1)}, u32[]{:S(2)}) copy-start(bf16[384,384]{1,0:T(8,128)(2,1)S(1)} %get-tuple-element.284.refs_9_.refs_10_.refs_11_.refs_12_) | copy-start | bytes 884740
  108.8 19.5 %collective-permute-start.38 = (bf16[224,384]{1,0:T(8,128)(2,1)S(1)}, bf16[224,384]{1,0:T(8,128)(2,1)S(1)}, u32[]{:S(2)}, u32[]{:S(2)}) collective-permute-start(bf16[224,384]{1,0:T(8,128)(2,1)S(1)} %dynamic-slice_bitcast_fusion.3.refs_0_), channel_id=1, source_target_pairs={{0,48},{16,0},{32,16},{48,32},{1,49},{17,1},{33,17},{49,33},{2,50}... | collective-permute-start | bytes 516104 | tf_op jit(solution)/shard_map/ppermute | solution.py:429
  124.1 6.2 %collective-permute-start.37 = (bf16[224,384]{1,0:T(8,128)(2,1)S(1)}, bf16[224,384]{1,0:T(8,128)(2,1)S(1)}, u32[]{:S(2)}, u32[]{:S(2)}) collective-permute-start(bf16[224,384]{1,0:T(8,128)(2,1)S(1)} %dynamic-slice_bitcast_fusion.3.refs_0_), channel_id=1, source_target_pairs={{0,32},{16,48},{32,0},{48,16},{1,33},{17,49},{33,1},{49,17},{2,34}... | collective-permute-start | bytes 516104 | tf_op jit(solution)/shard_map/ppermute | solution.py:429
  125.9 6.2 %collective-permute-start.36 = (bf16[224,384]{1,0:T(8,128)(2,1)S(1)}, bf16[224,384]{1,0:T(8,128)(2,1)S(1)}, u32[]{:S(2)}, u32[]{:S(2)}) collective-permute-start(bf16[224,384]{1,0:T(8,128)(2,1)S(1)} %dynamic-slice_bitcast_fusion.3.refs_0_), channel_id=1, source_target_pairs={{0,16},{16,32},{32,48},{48,0},{1,17},{17,33},{33,49},{49,1},{2,18}... | collective-permute-start | bytes 516104 | tf_op jit(solution)/shard_map/ppermute | solution.py:429
  128.4 20.3 %collective-permute-start.41 = (bf16[736,384]{1,0:T(8,128)(2,1)S(1)}, bf16[736,384]{1,0:T(8,128)(2,1)S(1)}, u32[]{:S(2)}, u32[]{:S(2)}) collective-permute-start(bf16[736,384]{1,0:T(8,128)(2,1)S(1)} %pad_maximum_fusion.1.refs_0_), channel_id=1, source_target_pairs={{0,48},{16,0},{32,16},{48,32},{1,49},{17,1},{33,17},{49,33},{2,50}... | collective-permute-start | bytes 1695752 | tf_op jit(solution)/shard_map/ppermute | solution.py:429
  130.2 19.1 %collective-permute-start.40 = (bf16[736,384]{1,0:T(8,128)(2,1)S(1)}, bf16[736,384]{1,0:T(8,128)(2,1)S(1)}, u32[]{:S(2)}, u32[]{:S(2)}) collective-permute-start(bf16[736,384]{1,0:T(8,128)(2,1)S(1)} %pad_maximum_fusion.1.refs_0_), channel_id=1, source_target_pairs={{0,32},{16,48},{32,0},{48,16},{1,33},{17,49},{33,1},{49,17},{2,34}... | collective-permute-start | bytes 1695752 | tf_op jit(solution)/shard_map/ppermute | solution.py:429
  132.1 25.8 %collective-permute-start.39 = (bf16[736,384]{1,0:T(8,128)(2,1)S(1)}, bf16[736,384]{1,0:T(8,128)(2,1)S(1)}, u32[]{:S(2)}, u32[]{:S(2)}) collective-permute-start(bf16[736,384]{1,0:T(8,128)(2,1)S(1)} %pad_maximum_fusion.1.refs_0_), channel_id=1, source_target_pairs={{0,16},{16,32},{32,48},{48,0},{1,17},{17,33},{33,49},{49,1},{2,18}... | collective-permute-start | bytes 1695752 | tf_op jit(solution)/shard_map/ppermute | solution.py:429
  148.6 26.4 %copy-start.8 = (f32[384,384]{1,0:T(8,128)}, f32[384,384]{1,0:T(8,128)S(1)}, u32[]{:S(2)}) copy-start(f32[384,384]{1,0:T(8,128)S(1)} %get-tuple-element.301.refs_17_) | copy-start | bytes 1769476
  148.6 26.4 %copy-start.9 = (f32[384,384]{1,0:T(8,128)}, f32[384,384]{1,0:T(8,128)S(1)}, u32[]{:S(2)}) copy-start(f32[384,384]{1,0:T(8,128)S(1)} %get-tuple-element.304.refs_20_) | copy-start | bytes 1769476
  148.6 26.5 %copy-start.16 = (bf16[384,384]{1,0:T(8,128)(2,1)}, bf16[384,384]{1,0:T(8,128)(2,1)S(1)}, u32[]{:S(2)}) copy-start(bf16[384,384]{1,0:T(8,128)(2,1)S(1)} %get-tuple-element.293.refs_12_.refs_13_) | copy-start | bytes 884740
  148.6 26.5 %copy-start.17 = (bf16[384,384]{1,0:T(8,128)(2,1)}, bf16[384,384]{1,0:T(8,128)(2,1)S(1)}, u32[]{:S(2)}) copy-start(bf16[384,384]{1,0:T(8,128)(2,1)S(1)} %get-tuple-element.292.refs_9_) | copy-start | bytes 884740
  148.6 60.6 %collective-permute-start.11 = (bf16[1536,384]{1,0:T(8,128)(2,1)}, bf16[1536,384]{1,0:T(8,128)(2,1)S(1)}, u32[]{:S(2)}, u32[]{:S(2)}) collective-permute-start(bf16[1536,384]{1,0:T(8,128)(2,1)} %bitcast_convert_fusion), channel_id=1, source_target_pairs={{4,20},{5,21},{6,22},{7,23},{8,24},{9,25},{10,26},{11,27},{12,28},... | collective-permute-start | bytes 3538952 | tf_op jit(solution)/shard_map/ppermute | solution.py:423
  149.4 62.5 %collective-permute-start.26 = (bf16[2048,128]{1,0:T(8,128)(2,1)S(1)}, bf16[2048,128]{1,0:T(8,128)(2,1)S(1)}, u32[]{:S(2)}, u32[]{:S(2)}) collective-permute-start(bf16[2048,128]{1,0:T(8,128)(2,1)S(1)} %pad_maximum_fusion.3), channel_id=1, source_target_pairs={{8,12},{11,13},{14,14},{24,28},{27,29},{30,30},{40,44},{43,45},{46... | collective-permute-start | bytes 1572872 | tf_op jit(solution)/shard_map/ppermute | solution.py:525
  157.9 54.0 %collective-permute-start.25 = (bf16[2048,128]{1,0:T(8,128)(2,1)S(1)}, bf16[2048,128]{1,0:T(8,128)(2,1)S(1)}, u32[]{:S(2)}, u32[]{:S(2)}) collective-permute-start(bf16[2048,128]{1,0:T(8,128)(2,1)S(1)} %pad_maximum_fusion.3), channel_id=1, source_target_pairs={{7,12},{10,13},{13,14},{23,28},{26,29},{29,30},{39,44},{42,45},{45... | collective-permute-start | bytes 1572872 | tf_op jit(solution)/shard_map/ppermute | solution.py:525
  175.0 29.3 %copy-start.10 = (bf16[768,384]{1,0:T(8,128)(2,1)}, bf16[768,384]{1,0:T(8,128)(2,1)S(1)}, u32[]{:S(2)}) copy-start(bf16[768,384]{1,0:T(8,128)(2,1)S(1)} %get-tuple-element.295.refs_10_) | copy-start | bytes 1769476
  175.0 29.3 %copy-start.11 = (f32[384,384]{1,0:T(8,128)}, f32[384,384]{1,0:T(8,128)S(1)}, u32[]{:S(2)}) copy-start(f32[384,384]{1,0:T(8,128)S(1)} %get-tuple-element.302.refs_18_) | copy-start | bytes 1769476
  175.0 29.3 %copy-start.12 = (f32[384,384]{1,0:T(8,128)}, f32[384,384]{1,0:T(8,128)S(1)}, u32[]{:S(2)}) copy-start(f32[384,384]{1,0:T(8,128)S(1)} %get-tuple-element.305.refs_21_) | copy-start | bytes 1769476
  175.0 29.2 %copy-start.18 = (bf16[384,384]{1,0:T(8,128)(2,1)}, bf16[384,384]{1,0:T(8,128)(2,1)S(1)}, u32[]{:S(2)}) copy-start(bf16[384,384]{1,0:T(8,128)(2,1)S(1)} %get-tuple-element.296.refs_15_.refs_14_) | copy-start | bytes 884740
  204.4 22.1 %collective-permute-start.24 = (bf16[2048,128]{1,0:T(8,128)(2,1)S(1)}, bf16[2048,128]{1,0:T(8,128)(2,1)S(1)}, u32[]{:S(2)}, u32[]{:S(2)}) collective-permute-start(bf16[2048,128]{1,0:T(8,128)(2,1)S(1)} %pad_maximum_fusion.3), channel_id=1, source_target_pairs={{5,11},{6,12},{9,13},{12,14},{15,15},{21,27},{22,28},{25,29},{28,3... | collective-permute-start | bytes 1572872 | tf_op jit(solution)/shard_map/ppermute | solution.py:525
  208.0 34.0 %collective-permute-start.23 = (bf16[2048,128]{1,0:T(8,128)(2,1)S(1)}, bf16[2048,128]{1,0:T(8,128)(2,1)S(1)}, u32[]{:S(2)}, u32[]{:S(2)}) collective-permute-start(bf16[2048,128]{1,0:T(8,128)(2,1)S(1)} %pad_maximum_fusion.3), channel_id=1, source_target_pairs={{4,11},{5,12},{8,13},{11,14},{14,15},{20,27},{21,28},{24,29},{27,3... | collective-permute-start | bytes 1572872 | tf_op jit(solution)/shard_map/ppermute | solution.py:525
  209.3 42.6 %collective-permute-start.22 = (bf16[2048,128]{1,0:T(8,128)(2,1)S(1)}, bf16[2048,128]{1,0:T(8,128)(2,1)S(1)}, u32[]{:S(2)}, u32[]{:S(2)}) collective-permute-start(bf16[2048,128]{1,0:T(8,128)(2,1)S(1)} %pad_maximum_fusion.3), channel_id=1, source_target_pairs={{3,11},{4,12},{7,13},{10,14},{13,15},{19,27},{20,28},{23,29},{26,3... | collective-permute-start | bytes 1572872 | tf_op jit(solution)/shard_map/ppermute | solution.py:525
  211.9 40.0 %copy-start.24 = (bf16[2048,128]{1,0:T(8,128)(2,1)}, bf16[2048,128]{1,0:T(8,128)(2,1)S(1)}, u32[]{:S(2)}) copy-start(bf16[2048,128]{1,0:T(8,128)(2,1)S(1)} %collective-permute-done.26.refs_4_) | copy-start | bytes 1572868
  211.9 30.0 %copy-start.25 = (bf16[2048,128]{1,0:T(8,128)(2,1)}, bf16[2048,128]{1,0:T(8,128)(2,1)S(1)}, u32[]{:S(2)}) copy-start(bf16[2048,128]{1,0:T(8,128)(2,1)S(1)} %collective-permute-done.25.refs_3_) | copy-start | bytes 1572868
  226.4 25.4 %copy-start.26 = (bf16[2048,128]{1,0:T(8,128)(2,1)}, bf16[2048,128]{1,0:T(8,128)(2,1)S(1)}, u32[]{:S(2)}) copy-start(bf16[2048,128]{1,0:T(8,128)(2,1)S(1)} %collective-permute-done.24.refs_2_) | copy-start | bytes 1572868
  (8 other events, 47.9 us)
Sparse Core Ops, SparseCore 0:
  58.4 77.4 all-gather.2

commit v3 on v2

--- a/solution.py
+++ b/solution.py
@@ -465,35 +465,62 @@
         return jnp.concatenate(diag_part(s) + offs, axis=0)
 
     def head_part(s):
-        return jnp.concatenate(diag_part(s) + [child_part(s)], axis=0)
-
-    rest = rest_part(0)
-    rest_got = [x_from0(rest_part(s), s, range(1, 4)) for s in range(1, 4)]
+        off = high[s * PIECE : (s + 1) * PIECE]
+        return jnp.concatenate(diag_part(s) + [child_part(s), off], axis=0)
+
+    def x_swap(value, m):
+        return lax.ppermute(value, "row", [(i, i ^ m) for i in range(4)])
+
+    def x_pairs(value, pairs, cols):
+        return lax.ppermute(value, grid, [(flat(p, c), flat(q, c)) for p, q in pairs for c in cols])
+
+    def z_pairs(value, pairs):
+        return lax.ppermute(value, "col", [(4 * p + b, 4 * q + b) for p, q in pairs for b in range(4)])
+
+    def halves(value):
+        n = value.shape[0] // 2
+        return value[:n], value[n:]
+
+    late_cols = (2, 3)
+    rest_two = x_pairs(jnp.concatenate([rest_part(2), rest_part(3)], axis=0), [(0, 3)], late_cols)
+    a12 = lax.psum(jnp.where(me == 0, high, jnp.zeros((), BF16)), "row")
     head = own_or(me == 0, head_part(0), *[x_from0(head_part(s), s, range(3)) for s in range(1, 4)])
+    child_one = x_swap(received, 1)
+    rest_two, rest_one, child_one = after((rest_two, rest_part(1), child_one), head)
+    for_two, for_three = halves(rest_two)
+    got = x_pairs(jnp.where(me == 0, rest_one, for_two), [(0, 1), (3, 2)], late_cols)
+    rest = jnp.where(me == 0, rest_part(0), jnp.where(me == 3, for_three, got))
+    pair = jnp.where(me % 2 == 0, jnp.stack([received, child_one]), jnp.stack([child_one, received]))
+    pair = pair.reshape(-1, BLK)
+    child_two = x_swap(pair, 3)
+
     head_z = own_or(col < 4, head, *[z_from0(head, s) for s in range(1, 4)])
-    head_y = by_source(head_z, y_shift, y, range(3))
-    g0 = jnp.concatenate([head_y[0]] + [h[DIAG:] for h in head_y[1:]], axis=0)
-    g0 = [g0] + [x_shift(g0, s) for s in range(1, 4)]
-    rest = own_or(me == 0, rest, *after(rest_got, head_z))
-    rest = own_or(col < 4, rest, *[z_from0(rest, s) for s in range(1, 4)])
-    rest = after(rest, head_y[0])
-    rest_y = by_source(rest, y_shift, y, range(1, 4))
-    g1 = rest_y[0][: DIAG + PIECE]
-    g1 = [g1] + [x_shift(g1, s) for s in range(1, 4)]
-    g23 = jnp.concatenate([rest_y[1][: DIAG + 2 * PIECE], rest_y[2]], axis=0)
-    g23 = [g23] + [x_shift(g23, s) for s in range(1, 4)]
-
-    column = jnp.concatenate(by_source(after(received, head_z), x_shift, me, range(4)), axis=0)
+    column = jnp.where(me < 2, jnp.concatenate([pair, child_two], axis=0), jnp.concatenate([child_two, pair], axis=0))
+    rest, column = after((rest, column), head_z)
     first = jnp.where(me == 3, 4, 0)
     chosen = lax.dynamic_slice_in_dim(column, first * BLK, 12 * BLK, 0)
     panel_wide = jnp.concatenate([high, chosen], axis=1)
-    wide = own_or(
-        col < 4, panel_wide[:PANEL], *[z_from0(panel_wide[s * PANEL : (s + 1) * PANEL], s) for s in range(1, 4)]
-    )
+    rest_z1 = z_pairs(rest, [(0, 1)])
+    wide_two = z_pairs(panel_wide[2 * PANEL :], [(0, 3)])
+
+    head_y = by_source(head_z, y_shift, y, range(3))
+    child = slice(DIAG, DIAG + PART)
+    g0 = jnp.concatenate([head_y[0][: DIAG + PART], head_y[1][child], head_y[2][child]], axis=0)
+    g1 = jnp.concatenate([head_y[1][:DIAG], head_y[1][DIAG + PART :]], axis=0)
+    g01 = jnp.concatenate([g0, g1], axis=0)
+    rest_z1, wide_two = after((rest_z1, wide_two), head_y[0])
+    z = col // 4
+    rest = jnp.where(z == 0, rest, rest_z1)
+    rest_z2 = z_pairs(rest, [(0, 3), (1, 2)])
+    for_two, for_three = halves(wide_two)
+    wide_got = z_pairs(jnp.where(z == 0, panel_wide[PANEL : 2 * PANEL], for_two), [(0, 1), (3, 2)])
+    wide = jnp.where(z == 0, panel_wide[:PANEL], jnp.where(z == 3, for_three, wide_got))
+
+    g01 = [g01] + [x_shift(g01, s) for s in range(1, 4)]
+    rest = jnp.where(z < 2, rest, rest_z2)
+    rest = after(rest, *g01)
+    rest_y = by_source(rest, y_shift, y, (2, 3))
     wide = lax.all_gather(wide, "col")
-    a12 = after(high, g0[0], g0[1])
-    got = [x_from0(a12, s, range(4, N_COL)) for s in range(1, 4)]
-    a12 = got[0] + got[1] + got[2]
 
     ids = jnp.full((N_COL, THICK), -1, jnp.int32)
     for c in SOURCES:
@@ -507,23 +534,29 @@
 
     ups, invs, lows, mines = [], [], [], []
     flat_invs = []
-    thick = None
+    def contribution_column(value, j):
+        pairs = [(SOURCES[c][j], c) for c in SOURCES if j < len(SOURCES[c])]
+        return lax.ppermute(value, "col", pairs)
+
+    head_rows = g01
+    thick = []
     for k in range(PANELS):
-        pieces = [g0, g1, g23, g23][k]
-        base = DIAG + 2 * PIECE if k == 3 else 0
-        ih, il, up, low, mine_out = panel_call(k, base, info, index_map, pieces, g0, ups, flat_invs)
+        if k < 2:
+            pieces = head_rows
+        else:
+            piece = after(rest_y[k - 2][: DIAG + k * PIECE], invs[k - 2])
+            pieces = [piece] + [x_shift(piece, s) for s in range(1, 4)]
+        if k >= 2:
+            late = after(column, invs[k - 1])
+            thick += [contribution_column(late, j) for j in ((0, 1) if k == 2 else (2, 3, 4))]
+        base = DIAG + 3 * PART if k == 1 else 0
+        ih, il, up, low, mine_out = panel_call(k, base, info, index_map, pieces, head_rows, ups, flat_invs)
         flat_invs += [ih, il]
         ups.append(up)
         invs.append(ih)
         lows.append(low)
         mines.append(mine_out)
-        if k == 0:
-            late = after(column, ih)
-            thick = []
-            for j in range(THICK):
-                pairs = [(SOURCES[c][j], c) for c in SOURCES if j < len(SOURCES[c])]
-                thick.append(lax.ppermute(late, "col", pairs))
-    out = tail_call(info, index_map, front, a12, wide, thick, g0, ups[1:], invs, lows, mines[1:])
+    out = tail_call(info, index_map, front, a12, wide, thick, head_rows, ups[1:], invs, lows, mines[1:])
     return out[None]
 
 

time: 291 us -> 284 us (0.976)
  the two profiles are of different devices: /device:TPU:101 before, /device:TPU:46 now
where the time goes in v3:
time: 284 us; the launch traced here: 281 us
  Pallas kernels  103 us (36%)
  waiting for transfers between devices  69.1 us (24%)
  starting transfers between devices  62.9 us (22%)
  local copies, waits for them, and re-layouts  16.8 us (6%)
  between operations  15.6 us (5%)
  other arithmetic  13.4 us (5%)
    pallas_call x4, Pallas kernels, panel_call(): pl.pallas_call(functools.partial(panel_kernel, k, base), out_shape=[jax.S...  73.4 us
    pallas_call x1, Pallas kernels, tail_call(): pl.pallas_call(tail_kernel, out_shape=jax.ShapeDtypeStruct((LEAD, PANEL),...  29.3 us
    ppermute x4, waiting for transfers between devices, z_pairs(): lax.ppermute(value, 'col', [(4 * p + b, 4 * q + b) for p, q in pairs for...  28.7 us
    ppermute x6, waiting for transfers between devices, y_shift(): lax.ppermute(value, 'col', [(4 * z + b, 4 * z + (b + s) % 4) for z in ran...  16.6 us
    ppermute x5, starting transfers between devices, contribution_column(): return lax.ppermute(value, 'col', pairs)  16.4 us
    ppermute x6, starting transfers between devices, y_shift(): lax.ppermute(value, 'col', [(4 * z + b, 4 * z + (b + s) % 4) for z in ran...  15.6 us
    ppermute x9, starting transfers between devices, x_shift(): return lax.ppermute(value, 'row', [(i, (i + s) % 4) for i in range(4)])  14.9 us
    ppermute x3, waiting for transfers between devices, z_from0(): return lax.ppermute(value, 'col', [(b, 4 * s + b) for b in range(4)])  14.7 us
  transfers between devices with their start and end apart: 37, of which 12 were waited for; matrix products, arithmetic and copies ran while one was open for 8% of the time, Pallas kernels for 26%

profile of v3, /device:TPU:46, one launch (start us, length us, event | category | flops | bytes accessed | tf_op | source)
XLA Modules:
  0.0 280.5 jit_solution(9070689560611774309)
XLA Ops:
  7.4 1.3 dynamic-slice_bitcast_fusion
  9.8 0.9 dynamic-slice_bitcast_fusion.6
  13.3 1.2 broadcast_select_fusion
  20.6 0.9 fusion.15
  21.5 0.8 collective-permute-start.4
  22.3 0.7 pad_maximum_fusion.3
  23.7 0.7 pad_maximum_fusion.5
  25.1 0.9 collective-permute-start.2
  27.5 1.3 collective-permute-start.8
  28.8 2.5 collective-permute-done.2
  31.3 1.0 maximum_select_fusion.2
  33.6 14.7 %collective-permute-done.8 = bf16[256,384]{1,0:T(8,128)(2,1)S(1)} collective-permute-done((bf16[256,384]{1,0:T(8,128)(2,1)S(1)}, bf16[256,384]{1,0:T(8,128)(2,1)S(1)}, u32[]{:S(2)}, u32[]{:S(2)}) %collective-permute-start.8) | collective-permute-done | bytes 196640 | tf_op jit(solution)/shard_map/ppermute | solution.py:426
  48.4 1.0 maximum_select_fusion
  49.4 1.0 constant_dynamic-slice_fusion.1
  50.5 1.0 fusion
  51.4 0.7 collective-permute-start.12
  52.2 1.3 collective-permute-start.11
  53.5 9.6 %collective-permute-done.11 = bf16[416,384]{1,0:T(8,128)(2,1)S(1)} collective-permute-done((bf16[416,384]{1,0:T(8,128)(2,1)S(1)}, bf16[416,384]{1,0:T(8,128)(2,1)S(1)}, u32[]{:S(2)}, u32[]{:S(2)}) %collective-permute-start.11) | collective-permute-done | bytes 319520 | tf_op jit(solution)/shard_map/ppermute | solution.py:478
  63.2 0.7 copy-done.25
  63.9 0.9 fusion.1
  64.8 1.3 collective-permute-start.13
  66.1 15.4 %collective-permute-done.13 = bf16[384,512]{1,0:T(8,128)(2,1)S(1)} collective-permute-done((bf16[384,512]{1,0:T(8,128)(2,1)}, bf16[384,512]{1,0:T(8,128)(2,1)S(1)}, u32[]{:S(2)}, u32[]{:S(2)}) %collective-permute-start.13) | collective-permute-done | bytes 393248 | tf_op jit(solution)/shard_map/ppermute | solution.py:478
  81.5 0.9 maximum_select_fusion.1
  83.1 10.3 %collective-permute-start.15 = (bf16[256,384]{1,0:T(8,128)(2,1)S(1)}, bf16[256,384]{1,0:T(8,128)(2,1)S(1)}, u32[]{:S(2)}, u32[]{:S(2)}) collective-permute-start(bf16[256,384]{1,0:T(8,128)(2,1)S(1)} %add_add_fusion), channel_id=1, source_target_pairs={{0,2},{1,3},{2,0},{3,1},{4,6},{5,7},{6,4},{7,5},{8,10},{9,11},{10,... | collective-permute-start | bytes 589832 | tf_op jit(solution)/shard_map/ppermute | solution.py:432
  93.3 0.7 maximum_bitcast_fusion
  94.7 2.9 %collective-permute-done.16 = bf16[256,384]{1,0:T(8,128)(2,1)S(1)} collective-permute-done((bf16[256,384]{1,0:T(8,128)(2,1)S(1)}, bf16[256,384]{1,0:T(8,128)(2,1)S(1)}, u32[]{:S(2)}, u32[]{:S(2)}) %collective-permute-start.16) | collective-permute-done | bytes 196640 | tf_op jit(solution)/shard_map/ppermute | solution.py:432
  97.6 2.3 collective-permute-done.15
  99.9 0.7 collective-permute-done.14
  100.9 5.1 %collective-permute-start.22 = (bf16[416,384]{1,0:T(8,128)(2,1)S(1)}, bf16[416,384]{1,0:T(8,128)(2,1)S(1)}, u32[]{:S(2)}, u32[]{:S(2)}) collective-permute-start(bf16[416,384]{1,0:T(8,128)(2,1)S(1)} %broadcast_select_fusion.1), channel_id=1, source_target_pairs={{0,12},{1,13},{2,14},{3,15},{4,8},{5,9},{6,10},{7,11},{16,28},{17,... | collective-permute-start | bytes 958472 | tf_op jit(solution)/shard_map/ppermute | solution.py:478
  106.1 1.5 collective-permute-start.19
  107.6 1.5 collective-permute-start.18
  109.1 2.5 collective-permute-start.17
  111.7 0.7 bitcast_select_fusion.1
  112.5 3.7 %collective-permute-done.22 = bf16[416,384]{1,0:T(8,128)(2,1)S(1)} collective-permute-done((bf16[416,384]{1,0:T(8,128)(2,1)S(1)}, bf16[416,384]{1,0:T(8,128)(2,1)S(1)}, u32[]{:S(2)}, u32[]{:S(2)}) %collective-permute-start.22) | collective-permute-done | bytes 319520 | tf_op jit(solution)/shard_map/ppermute | solution.py:478
  116.2 1.8 collective-permute-done.19.refs_3_.refs_7_.refs_8_
  118.0 4.7 %collective-permute-done.18.refs_2_.refs_6_.refs_7_ = bf16[448,384]{1,0:T(8,128)(2,1)S(1)} collective-permute-done((bf16[448,384]{1,0:T(8,128)(2,1)S(1)}, bf16[448,384]{1,0:T(8,128)(2,1)S(1)}, u32[]{:S(2)}, u32[]{:S(2)}) %collective-permute-start.18) | collective-permute-done | bytes 344096 | tf_op jit(solution)/shard_map/ppermute | solution.py:429
  122.7 1.5 collective-permute-start.25
  124.2 1.5 collective-permute-start.24
  125.7 1.8 collective-permute-start.23
  127.5 14.1 %panel0.1 = (bf16[384,384]{1,0:T(8,128)(2,1)S(1)}, bf16[384,384]{1,0:T(8,128)(2,1)S(1)}, bf16[16,384]{1,0:T(8,128)(2,1)S(1)}, f32[384,384]{1,0:T(8,128)S(1)}, f32[384,384]{1,0:T(8,128)}) custom-call(s32[16]{0:T(128)S(1)} %concatenate.122.info, s32[16]{0:T(128)S(1)} %bitcast.65, bf16[448,384]{1,0:T(8,128)(2,1)S(1)} %fusion.7.refs_0_.refs_4_.refs_5_, ...), custom_call_target="tpu_custom_call" | custom-call | flops 10000000000 | bytes 1000000 | tf_op jit(solution)/shard_map/panel0/pallas_call | solution.py:210
  141.6 6.8 %collective-permute-done.24 = bf16[416,384]{1,0:T(8,128)(2,1)S(1)} collective-permute-done((bf16[416,384]{1,0:T(8,128)(2,1)S(1)}, bf16[416,384]{1,0:T(8,128)(2,1)S(1)}, u32[]{:S(2)}, u32[]{:S(2)}) %collective-permute-start.24) | collective-permute-done | bytes 319520 | tf_op jit(solution)/shard_map/ppermute | solution.py:432
  148.4 3.8 %collective-permute-done.23 = bf16[416,384]{1,0:T(8,128)(2,1)S(1)} collective-permute-done((bf16[416,384]{1,0:T(8,128)(2,1)S(1)}, bf16[416,384]{1,0:T(8,128)(2,1)S(1)}, u32[]{:S(2)}, u32[]{:S(2)}) %collective-permute-start.23) | collective-permute-done | bytes 319520 | tf_op jit(solution)/shard_map/ppermute | solution.py:432
  152.5 2.7 collective-permute-start.28
  155.2 1.4 collective-permute-start.27
  156.6 1.4 collective-permute-start.26
  158.0 14.8 %panel1.1 = (bf16[384,384]{1,0:T(8,128)(2,1)S(1)}, bf16[384,384]{1,0:T(8,128)(2,1)S(1)}, bf16[384,384]{1,0:T(8,128)(2,1)S(1)}, f32[384,384]{1,0:T(8,128)S(1)}, f32[384,384]{1,0:T(8,128)S(1)}) custom-call(s32[16]{0:T(128)S(1)} %concatenate.122.info, s32[16]{0:T(128)S(1)} %bitcast.66, bf16[448,384]{1,0:T(8,128)(2,1)S(1)} %fusion.7.refs_0_.refs_4_.refs_5_, ...), custom_call_target="tpu_custom_call" | custom-call | flops 10000000000 | bytes 1000000 | tf_op jit(solution)/shard_map/panel1/pallas_call | solution.py:210
  172.8 0.8 copy-done.9
  173.6 3.2 %collective-permute-start.21 = (bf16[2048,128]{1,0:T(8,128)(2,1)}, bf16[2048,128]{1,0:T(8,128)(2,1)}, u32[]{:S(2)}, u32[]{:S(2)}) collective-permute-start(bf16[2048,128]{1,0:T(8,128)(2,1)} %maximum_select_fusion), channel_id=1, source_target_pairs={{4,11},{5,12},{8,13},{11,14},{14,15},{20,27},{21,28},{24,29},{27,3... | collective-permute-start | bytes 1572872 | tf_op jit(solution)/shard_map/ppermute | solution.py:539
  176.8 1.5 collective-permute-start.20
  178.3 1.0 collective-permute-start.34
  179.3 0.7 collective-permute-start.33
  180.1 2.1 collective-permute-start.32
  182.1 15.8 %panel2.1 = (bf16[384,384]{1,0:T(8,128)(2,1)S(1)}, bf16[384,384]{1,0:T(8,128)(2,1)S(1)}, bf16[768,384]{1,0:T(8,128)(2,1)S(1)}, f32[384,384]{1,0:T(8,128)S(1)}, f32[384,384]{1,0:T(8,128)S(1)}) custom-call(s32[16]{0:T(128)S(1)} %concatenate.122.info, s32[16]{0:T(128)S(1)} %bitcast.67, bf16[320,384]{1,0:T(8,128)(2,1)S(1)} %dynamic-slice_bitcast_fusion.2.refs_0_, ...), custom_call_target="tpu_custom_call" | custom-call | flops 10000000000 | bytes 1000000 | tf_op jit(solution)/shard_map/panel2/pallas_call | solution.py:210
  197.9 0.8 copy-done.11
  198.7 0.8 copy-done.12
  199.6 1.5 collective-permute-start.31
  201.0 1.5 collective-permute-start.30
  202.5 8.8 %collective-permute-start.29 = (bf16[2048,128]{1,0:T(8,128)(2,1)}, bf16[2048,128]{1,0:T(8,128)(2,1)}, u32[]{:S(2)}, u32[]{:S(2)}) collective-permute-start(bf16[2048,128]{1,0:T(8,128)(2,1)} %maximum_select_fusion), channel_id=1, source_target_pairs={{5,11},{6,12},{9,13},{12,14},{15,15},{21,27},{22,28},{25,29},{28,3... | collective-permute-start | bytes 1572872 | tf_op jit(solution)/shard_map/ppermute | solution.py:539
  211.3 28.8 %panel3.1 = (bf16[384,384]{1,0:T(8,128)(2,1)S(1)}, bf16[384,384]{1,0:T(8,128)(2,1)}, bf16[1152,384]{1,0:T(8,128)(2,1)S(1)}, f32[384,384]{1,0:T(8,128)S(1)}, f32[384,384]{1,0:T(8,128)S(1)}) custom-call(s32[16]{0:T(128)S(1)} %concatenate.122.info, s32[16]{0:T(128)S(1)} %bitcast.68, bf16[416,384]{1,0:T(8,128)(2,1)S(1)} %dynamic-slice_bitcast_fusion.1.refs_0_, ...), custom_call_target="tpu_custom_call" | custom-call | flops 10000000000 | bytes 1000000 | tf_op jit(solution)/shard_map/panel3/pallas_call | solution.py:210
  240.1 1.0 copy-done.6
  241.1 0.8 copy-done.13
  241.9 0.8 copy-done.14
  242.8 0.7 copy-done.19
  243.6 29.3 %tail.1 = f32[1536,384]{1,0:T(8,128)} custom-call(s32[16]{0:T(128)} %copy-done.2, s32[16]{0:T(128)} %bitcast.63, f32[1536,384]{1,0:T(8,128)} %bitcast.69, bf16[1536,384]{1,0:T(8,128)(2,1)} %all-reduce.2.cloned.1.call-done.a12, bf16[16,384,512]{2,1,0:T(8,128)(2,1)} %bitcast.81, bf16[2048,128]{1,0:T(8,128)(2,1)} %collective-permute-done.20.refs_0_, ...), custom_call_target="tpu_custom_call" | custom-call | flops 7000000000 | bytes 20000000 | tf_op jit(solution)/shard_map/tail/pallas_call | solution.py:395
  (131 shorter events, 16.1 us)
Async XLA Ops:
  7.4 236.1 %all-reduce.2.cloned.1.call-start = ((), (), s32[]{:S(2)}) async-start(), calls=%async_computation | async-start | bytes 2359296 | tf_op jit(solution)/shard_map/psum | solution.py:486
  7.4 13.2 %collective-permute-start.1 = (bf16[512,128]{1,0:T(8,128)(2,1)}, bf16[512,128]{1,0:T(8,128)(2,1)}, u32[]{:S(2)}, u32[]{:S(2)}) collective-permute-start(bf16[512,128]{1,0:T(8,128)(2,1)} %bitcast.82), channel_id=1, source_target_pairs={{0,64},{64,0},{1,65},{65,1},{2,66},{66,2},{3,67},{67,3},{4,68},{68... | collective-permute-start | bytes 393224 | tf_op jit(solution)/shard_map/ppermute | solution.py:447
  7.4 5.9 %copy-start.20 = (f32[1,1536,384]{2,1,0:T(8,128)S(1)}, f32[1,1536,384]{2,1,0:T(8,128)}, u32[]{:S(2)}) copy-start(f32[1,1536,384]{2,1,0:T(8,128)} %param.45) | copy-start | bytes 7077892
  14.5 2.0 copy-start.27
  14.5 2.0 copy-start.30
  15.2 9.2 %copy-start.23 = (bf16[416,384]{1,0:T(8,128)(2,1)}, bf16[416,384]{1,0:T(8,128)(2,1)S(1)}, u32[]{:S(2)}) copy-start(bf16[416,384]{1,0:T(8,128)(2,1)S(1)} %get-tuple-element.357) | copy-start | bytes 958468
  16.5 9.5 %copy-start.28 = (bf16[64,384]{1,0:T(8,128)(2,1)S(1)}, bf16[64,384]{1,0:T(8,128)(2,1)}, u32[]{:S(2)}) copy-start(bf16[64,384]{1,0:T(8,128)(2,1)} %get-tuple-element.382) | copy-start | bytes 147460
  16.5 9.5 %copy-start.29 = (bf16[64,384]{1,0:T(8,128)(2,1)S(1)}, bf16[64,384]{1,0:T(8,128)(2,1)}, u32[]{:S(2)}) copy-start(bf16[64,384]{1,0:T(8,128)(2,1)} %get-tuple-element.344) | copy-start | bytes 147460
  19.9 11.4 %collective-permute-start = (bf16[832,384]{1,0:T(8,128)(2,1)}, bf16[832,384]{1,0:T(8,128)(2,1)S(1)}, u32[]{:S(2)}, u32[]{:S(2)}) collective-permute-start(bf16[832,384]{1,0:T(8,128)(2,1)} %slice_dynamic-update-slice_fusion.2), channel_id=1, source_target_pairs={{2,50},{3,51},{66,114},{67,115}} | collective-permute-start | bytes 1916936 | tf_op jit(solution)/shard_map/ppermute | solution.py:475
  21.5 11.4 %copy-start.22 = (bf16[416,384]{1,0:T(8,128)(2,1)S(1)}, bf16[416,384]{1,0:T(8,128)(2,1)}, u32[]{:S(2)}) copy-start(bf16[416,384]{1,0:T(8,128)(2,1)} %copy-done.21) | copy-start | bytes 958468
  21.5 4.5 %collective-permute-start.4 = (bf16[256,384]{1,0:T(8,128)(2,1)S(1)}, bf16[256,384]{1,0:T(8,128)(2,1)S(1)}, u32[]{:S(2)}, u32[]{:S(2)}) collective-permute-start(bf16[256,384]{1,0:T(8,128)(2,1)S(1)} %pad_maximum_fusion.4), channel_id=1, source_target_pairs={{0,32},{1,33},{2,34},{64,96},{65,97},{66,98}} | collective-permute-start | bytes 589832 | tf_op jit(solution)/shard_map/ppermute | solution.py:423
  23.0 3.0 %collective-permute-start.3 = (bf16[256,384]{1,0:T(8,128)(2,1)}, bf16[256,384]{1,0:T(8,128)(2,1)S(1)}, u32[]{:S(2)}, u32[]{:S(2)}) collective-permute-start(bf16[256,384]{1,0:T(8,128)(2,1)} %pad_maximum_fusion.3), channel_id=1, source_target_pairs={{0,16},{1,17},{2,18},{64,80},{65,81},{66,82}} | collective-permute-start | bytes 589832 | tf_op jit(solution)/shard_map/ppermute | solution.py:423
  24.4 1.6 collective-permute-start.5
  25.1 6.2 %collective-permute-start.2 = (bf16[512,128]{1,0:T(8,128)(2,1)}, bf16[512,128]{1,0:T(8,128)(2,1)S(1)}, u32[]{:S(2)}, u32[]{:S(2)}) collective-permute-start(bf16[512,128]{1,0:T(8,128)(2,1)} %collective-permute-done.1), channel_id=1, source_target_pairs={{0,16},{16,0},{32,48},{48,32},{1,17},{17,1},{33,49},{49,33},{2,18}... | collective-permute-start | bytes 393224 | tf_op jit(solution)/shard_map/ppermute | solution.py:472
  26.1 7.5 %collective-permute-start.10 = (bf16[256,384]{1,0:T(8,128)(2,1)S(1)}, bf16[256,384]{1,0:T(8,128)(2,1)S(1)}, u32[]{:S(2)}, u32[]{:S(2)}) collective-permute-start(bf16[256,384]{1,0:T(8,128)(2,1)S(1)} %fusion.4), channel_id=1, source_target_pairs={{0,12},{1,13},{2,14},{3,15},{16,28},{17,29},{18,30},{19,31},{32,44... | collective-permute-start | bytes 589832 | tf_op jit(solution)/shard_map/ppermute | solution.py:426
  26.8 6.8 %collective-permute-start.9 = (bf16[256,384]{1,0:T(8,128)(2,1)S(1)}, bf16[256,384]{1,0:T(8,128)(2,1)S(1)}, u32[]{:S(2)}, u32[]{:S(2)}) collective-permute-start(bf16[256,384]{1,0:T(8,128)(2,1)S(1)} %fusion.4), channel_id=1, source_target_pairs={{0,8},{1,9},{2,10},{3,11},{16,24},{17,25},{18,26},{19,27},{32,40},... | collective-permute-start | bytes 589832 | tf_op jit(solution)/shard_map/ppermute | solution.py:426
  27.5 20.8 %collective-permute-start.8 = (bf16[256,384]{1,0:T(8,128)(2,1)S(1)}, bf16[256,384]{1,0:T(8,128)(2,1)S(1)}, u32[]{:S(2)}, u32[]{:S(2)}) collective-permute-start(bf16[256,384]{1,0:T(8,128)(2,1)S(1)} %fusion.4), channel_id=1, source_target_pairs={{0,4},{1,5},{2,6},{3,7},{16,20},{17,21},{18,22},{19,23},{32,36},{3... | collective-permute-start | bytes 589832 | tf_op jit(solution)/shard_map/ppermute | solution.py:426
  32.3 17.1 %copy-start.24 = (bf16[416,384]{1,0:T(8,128)(2,1)S(1)}, bf16[416,384]{1,0:T(8,128)(2,1)}, u32[]{:S(2)}) copy-start(bf16[416,384]{1,0:T(8,128)(2,1)} %copy-done.23) | copy-start | bytes 958468
  32.3 16.1 %collective-permute-start.7 = (bf16[1024,128]{1,0:T(8,128)(2,1)S(1)}, bf16[1024,128]{1,0:T(8,128)(2,1)S(1)}, u32[]{:S(2)}, u32[]{:S(2)}) collective-permute-start(bf16[1024,128]{1,0:T(8,128)(2,1)S(1)} %bitcast.71), channel_id=1, source_target_pairs={{0,48},{16,32},{32,16},{48,0},{1,49},{17,33},{33,17},{49,1},{2,50}... | collective-permute-start | bytes 786440 | tf_op jit(solution)/shard_map/ppermute | solution.py:472
  32.9 16.4 %collective-permute-start.6 = (bf16[416,384]{1,0:T(8,128)(2,1)S(1)}, bf16[416,384]{1,0:T(8,128)(2,1)S(1)}, u32[]{:S(2)}, u32[]{:S(2)}) collective-permute-start(bf16[416,384]{1,0:T(8,128)(2,1)S(1)} %slice_select_fusion), channel_id=1, source_target_pairs={{2,18},{3,19},{50,34},{51,35},{66,82},{67,83},{114,98},{115,99}} | collective-permute-start | bytes 958472 | tf_op jit(solution)/shard_map/ppermute | solution.py:475
  51.4 11.7 %collective-permute-start.12 = (bf16[768,512]{1,0:T(8,128)(2,1)}, bf16[768,512]{1,0:T(8,128)(2,1)S(1)}, u32[]{:S(2)}, u32[]{:S(2)}) collective-permute-start(bf16[768,512]{1,0:T(8,128)(2,1)} %fusion), channel_id=1, source_target_pairs={{0,12},{1,13},{2,14},{3,15},{16,28},{17,29},{18,30},{19,31},{32,44... | collective-permute-start | bytes 2359304 | tf_op jit(solution)/shard_map/ppermute | solution.py:478
  52.2 11.0 %collective-permute-start.11 = (bf16[416,384]{1,0:T(8,128)(2,1)S(1)}, bf16[416,384]{1,0:T(8,128)(2,1)S(1)}, u32[]{:S(2)}, u32[]{:S(2)}) collective-permute-start(bf16[416,384]{1,0:T(8,128)(2,1)S(1)} %select_select_fusion), channel_id=1, source_target_pairs={{0,4},{1,5},{2,6},{3,7},{16,20},{17,21},{18,22},{19,23},{32,36},{3... | collective-permute-start | bytes 958472 | tf_op jit(solution)/shard_map/ppermute | solution.py:478
  53.5 190.1 %all-gather.3.cloned.1.call-start = ((), (), s32[]{:S(2)}) async-start(), calls=%async_computation.1 | async-start | bytes 6684672 | tf_op jit(solution)/shard_map/all_gather | solution.py:523
  64.8 16.7 %collective-permute-start.13 = (bf16[384,512]{1,0:T(8,128)(2,1)}, bf16[384,512]{1,0:T(8,128)(2,1)S(1)}, u32[]{:S(2)}, u32[]{:S(2)}) collective-permute-start(bf16[384,512]{1,0:T(8,128)(2,1)} %fusion.1), channel_id=1, source_target_pairs={{0,4},{1,5},{2,6},{3,7},{12,8},{13,9},{14,10},{15,11},{16,20},{17,... | collective-permute-start | bytes 1179656 | tf_op jit(solution)/shard_map/ppermute | solution.py:478
  66.1 27.9 %copy-start = (s32[1,16]{1,0:T(1,128)S(1)}, s32[1,16]{1,0:T(1,128)}, u32[]{:S(2)}) copy-start(s32[1,16]{1,0:T(1,128)} %param.47) | copy-start | bytes 196
  82.5 15.1 %collective-permute-start.16 = (bf16[256,384]{1,0:T(8,128)(2,1)S(1)}, bf16[256,384]{1,0:T(8,128)(2,1)S(1)}, u32[]{:S(2)}, u32[]{:S(2)}) collective-permute-start(bf16[256,384]{1,0:T(8,128)(2,1)S(1)} %add_add_fusion), channel_id=1, source_target_pairs={{0,3},{1,0},{2,1},{3,2},{4,7},{5,4},{6,5},{7,6},{8,11},{9,8},{10,9... | collective-permute-start | bytes 589832 | tf_op jit(solution)/shard_map/ppermute | solution.py:432
  83.1 16.8 %collective-permute-start.15 = (bf16[256,384]{1,0:T(8,128)(2,1)S(1)}, bf16[256,384]{1,0:T(8,128)(2,1)S(1)}, u32[]{:S(2)}, u32[]{:S(2)}) collective-permute-start(bf16[256,384]{1,0:T(8,128)(2,1)S(1)} %add_add_fusion), channel_id=1, source_target_pairs={{0,2},{1,3},{2,0},{3,1},{4,6},{5,7},{6,4},{7,5},{8,10},{9,11},{10,... | collective-permute-start | bytes 589832 | tf_op jit(solution)/shard_map/ppermute | solution.py:432
  93.3 7.3 %collective-permute-start.14 = (bf16[256,384]{1,0:T(8,128)(2,1)S(1)}, bf16[256,384]{1,0:T(8,128)(2,1)S(1)}, u32[]{:S(2)}, u32[]{:S(2)}) collective-permute-start(bf16[256,384]{1,0:T(8,128)(2,1)S(1)} %add_add_fusion), channel_id=1, source_target_pairs={{0,1},{1,2},{2,3},{3,0},{4,5},{5,6},{6,7},{7,4},{8,9},{9,10},{10,1... | collective-permute-start | bytes 589832 | tf_op jit(solution)/shard_map/ppermute | solution.py:432
  94.0 6.9 %copy-start.26 = (bf16[416,384]{1,0:T(8,128)(2,1)S(1)}, bf16[416,384]{1,0:T(8,128)(2,1)}, u32[]{:S(2)}) copy-start(bf16[416,384]{1,0:T(8,128)(2,1)} %copy-done.25) | copy-start | bytes 958468
  100.9 15.2 %collective-permute-start.22 = (bf16[416,384]{1,0:T(8,128)(2,1)S(1)}, bf16[416,384]{1,0:T(8,128)(2,1)S(1)}, u32[]{:S(2)}, u32[]{:S(2)}) collective-permute-start(bf16[416,384]{1,0:T(8,128)(2,1)S(1)} %broadcast_select_fusion.1), channel_id=1, source_target_pairs={{0,12},{1,13},{2,14},{3,15},{4,8},{5,9},{6,10},{7,11},{16,28},{17,... | collective-permute-start | bytes 958472 | tf_op jit(solution)/shard_map/ppermute | solution.py:478
  106.1 105.2 %copy-start.1 = (bf16[448,384]{1,0:T(8,128)(2,1)}, bf16[448,384]{1,0:T(8,128)(2,1)S(1)}, u32[]{:S(2)}) copy-start(bf16[448,384]{1,0:T(8,128)(2,1)S(1)} %fusion.7.refs_0_.refs_4_.refs_5_) | copy-start | bytes 1032196
  106.1 11.9 %collective-permute-start.19 = (bf16[448,384]{1,0:T(8,128)(2,1)S(1)}, bf16[448,384]{1,0:T(8,128)(2,1)S(1)}, u32[]{:S(2)}, u32[]{:S(2)}) collective-permute-start(bf16[448,384]{1,0:T(8,128)(2,1)S(1)} %fusion.7.refs_0_.refs_4_.refs_5_), channel_id=1, source_target_pairs={{0,48},{16,0},{32,16},{48,32},{1,49},{17,1},{33,17},{49,33},{2,50}... | collective-permute-start | bytes 1032200 | tf_op jit(solution)/shard_map/ppermute | solution.py:429
  107.6 15.1 %collective-permute-start.18 = (bf16[448,384]{1,0:T(8,128)(2,1)S(1)}, bf16[448,384]{1,0:T(8,128)(2,1)S(1)}, u32[]{:S(2)}, u32[]{:S(2)}) collective-permute-start(bf16[448,384]{1,0:T(8,128)(2,1)S(1)} %fusion.7.refs_0_.refs_4_.refs_5_), channel_id=1, source_target_pairs={{0,32},{16,48},{32,0},{48,16},{1,33},{17,49},{33,1},{49,17},{2,34}... | collective-permute-start | bytes 1032200 | tf_op jit(solution)/shard_map/ppermute | solution.py:429
  109.1 13.6 %collective-permute-start.17 = (bf16[448,384]{1,0:T(8,128)(2,1)S(1)}, bf16[448,384]{1,0:T(8,128)(2,1)S(1)}, u32[]{:S(2)}, u32[]{:S(2)}) collective-permute-start(bf16[448,384]{1,0:T(8,128)(2,1)S(1)} %fusion.7.refs_0_.refs_4_.refs_5_), channel_id=1, source_target_pairs={{0,16},{16,32},{32,48},{48,0},{1,17},{17,33},{33,49},{49,1},{2,18}... | collective-permute-start | bytes 1032200 | tf_op jit(solution)/shard_map/ppermute | solution.py:429
  112.5 98.8 %copy-start.2 = (s32[16]{0:T(128)}, s32[16]{0:T(128)S(1)}, u32[]{:S(2)}) copy-start(s32[16]{0:T(128)S(1)} %concatenate.122.info) | copy-start | bytes 196
  118.0 93.2 %copy-start.3 = (bf16[448,384]{1,0:T(8,128)(2,1)}, bf16[448,384]{1,0:T(8,128)(2,1)S(1)}, u32[]{:S(2)}) copy-start(bf16[448,384]{1,0:T(8,128)(2,1)S(1)} %collective-permute-done.19.refs_3_.refs_7_.refs_8_) | copy-start | bytes 1032196
  122.7 88.6 %copy-start.4 = (bf16[448,384]{1,0:T(8,128)(2,1)}, bf16[448,384]{1,0:T(8,128)(2,1)S(1)}, u32[]{:S(2)}) copy-start(bf16[448,384]{1,0:T(8,128)(2,1)S(1)} %collective-permute-done.18.refs_2_.refs_6_.refs_7_) | copy-start | bytes 1032196
  122.7 88.6 %copy-start.5 = (bf16[448,384]{1,0:T(8,128)(2,1)}, bf16[448,384]{1,0:T(8,128)(2,1)S(1)}, u32[]{:S(2)}) copy-start(bf16[448,384]{1,0:T(8,128)(2,1)S(1)} %collective-permute-done.17.refs_1_.refs_5_.refs_6_) | copy-start | bytes 1032196
  122.7 18.9 %collective-permute-start.25 = (bf16[416,384]{1,0:T(8,128)(2,1)S(1)}, bf16[416,384]{1,0:T(8,128)(2,1)S(1)}, u32[]{:S(2)}, u32[]{:S(2)}) collective-permute-start(bf16[416,384]{1,0:T(8,128)(2,1)S(1)} %broadcast_select_fusion.2), channel_id=1, source_target_pairs={{0,3},{1,0},{2,1},{3,2},{4,7},{5,4},{6,5},{7,6},{8,11},{9,8},{10,9... | collective-permute-start | bytes 958472 | tf_op jit(solution)/shard_map/ppermute | solution.py:432
  124.2 24.2 %collective-permute-start.24 = (bf16[416,384]{1,0:T(8,128)(2,1)S(1)}, bf16[416,384]{1,0:T(8,128)(2,1)S(1)}, u32[]{:S(2)}, u32[]{:S(2)}) collective-permute-start(bf16[416,384]{1,0:T(8,128)(2,1)S(1)} %broadcast_select_fusion.2), channel_id=1, source_target_pairs={{0,2},{1,3},{2,0},{3,1},{4,6},{5,7},{6,4},{7,5},{8,10},{9,11},{10,... | collective-permute-start | bytes 958472 | tf_op jit(solution)/shard_map/ppermute | solution.py:432
  125.7 26.5 %collective-permute-start.23 = (bf16[416,384]{1,0:T(8,128)(2,1)S(1)}, bf16[416,384]{1,0:T(8,128)(2,1)S(1)}, u32[]{:S(2)}, u32[]{:S(2)}) collective-permute-start(bf16[416,384]{1,0:T(8,128)(2,1)S(1)} %broadcast_select_fusion.2), channel_id=1, source_target_pairs={{0,1},{1,2},{2,3},{3,0},{4,5},{5,6},{6,7},{7,4},{8,9},{9,10},{10,1... | collective-permute-start | bytes 958472 | tf_op jit(solution)/shard_map/ppermute | solution.py:432
  141.6 10.8 %copy-start.7 = (f32[384,384]{1,0:T(8,128)}, f32[384,384]{1,0:T(8,128)S(1)}, u32[]{:S(2)}) copy-start(f32[384,384]{1,0:T(8,128)S(1)} %get-tuple-element.310.refs_16_) | copy-start | bytes 1769476
  141.6 69.7 %copy-start.15 = (bf16[384,384]{1,0:T(8,128)(2,1)}, bf16[384,384]{1,0:T(8,128)(2,1)S(1)}, u32[]{:S(2)}) copy-start(bf16[384,384]{1,0:T(8,128)(2,1)S(1)} %get-tuple-element.294.refs_9_.refs_10_.refs_11_.refs_12_) | copy-start | bytes 884740
  152.5 25.8 %collective-permute-start.28 = (bf16[320,384]{1,0:T(8,128)(2,1)S(1)}, bf16[320,384]{1,0:T(8,128)(2,1)S(1)}, u32[]{:S(2)}, u32[]{:S(2)}) collective-permute-start(bf16[320,384]{1,0:T(8,128)(2,1)S(1)} %dynamic-slice_bitcast_fusion.2.refs_0_), channel_id=1, source_target_pairs={{0,48},{16,0},{32,16},{48,32},{1,49},{17,1},{33,17},{49,33},{2,50}... | collective-permute-start | bytes 737288 | tf_op jit(solution)/shard_map/ppermute | solution.py:429
  155.2 24.1 %collective-permute-start.27 = (bf16[320,384]{1,0:T(8,128)(2,1)S(1)}, bf16[320,384]{1,0:T(8,128)(2,1)S(1)}, u32[]{:S(2)}, u32[]{:S(2)}) collective-permute-start(bf16[320,384]{1,0:T(8,128)(2,1)S(1)} %dynamic-slice_bitcast_fusion.2.refs_0_), channel_id=1, source_target_pairs={{0,32},{16,48},{32,0},{48,16},{1,33},{17,49},{33,1},{49,17},{2,34}... | collective-permute-start | bytes 737288 | tf_op jit(solution)/shard_map/ppermute | solution.py:429
  156.6 23.4 %collective-permute-start.26 = (bf16[320,384]{1,0:T(8,128)(2,1)S(1)}, bf16[320,384]{1,0:T(8,128)(2,1)S(1)}, u32[]{:S(2)}, u32[]{:S(2)}) collective-permute-start(bf16[320,384]{1,0:T(8,128)(2,1)S(1)} %dynamic-slice_bitcast_fusion.2.refs_0_), channel_id=1, source_target_pairs={{0,16},{16,32},{32,48},{48,0},{1,17},{17,33},{33,49},{49,1},{2,18}... | collective-permute-start | bytes 737288 | tf_op jit(solution)/shard_map/ppermute | solution.py:429
  172.7 0.8 copy-start.9
  173.6 24.3 %copy-start.8 = (f32[384,384]{1,0:T(8,128)}, f32[384,384]{1,0:T(8,128)S(1)}, u32[]{:S(2)}) copy-start(f32[384,384]{1,0:T(8,128)S(1)} %get-tuple-element.311.refs_17_) | copy-start | bytes 1769476
  173.6 37.7 %copy-start.16 = (bf16[384,384]{1,0:T(8,128)(2,1)}, bf16[384,384]{1,0:T(8,128)(2,1)S(1)}, u32[]{:S(2)}) copy-start(bf16[384,384]{1,0:T(8,128)(2,1)S(1)} %get-tuple-element.296.refs_12_.refs_13_) | copy-start | bytes 884740
  173.6 37.7 %copy-start.17 = (bf16[384,384]{1,0:T(8,128)(2,1)}, bf16[384,384]{1,0:T(8,128)(2,1)S(1)}, u32[]{:S(2)}) copy-start(bf16[384,384]{1,0:T(8,128)(2,1)S(1)} %get-tuple-element.301.refs_9_) | copy-start | bytes 884740
  173.6 69.9 %collective-permute-start.21 = (bf16[2048,128]{1,0:T(8,128)(2,1)}, bf16[2048,128]{1,0:T(8,128)(2,1)}, u32[]{:S(2)}, u32[]{:S(2)}) collective-permute-start(bf16[2048,128]{1,0:T(8,128)(2,1)} %maximum_select_fusion), channel_id=1, source_target_pairs={{4,11},{5,12},{8,13},{11,14},{14,15},{20,27},{21,28},{24,29},{27,3... | collective-permute-start | bytes 1572872 | tf_op jit(solution)/shard_map/ppermute | solution.py:539
  176.8 66.7 %collective-permute-start.20 = (bf16[2048,128]{1,0:T(8,128)(2,1)}, bf16[2048,128]{1,0:T(8,128)(2,1)}, u32[]{:S(2)}, u32[]{:S(2)}) collective-permute-start(bf16[2048,128]{1,0:T(8,128)(2,1)} %maximum_select_fusion), channel_id=1, source_target_pairs={{3,11},{4,12},{7,13},{10,14},{13,15},{19,27},{20,28},{23,29},{26,3... | collective-permute-start | bytes 1572872 | tf_op jit(solution)/shard_map/ppermute | solution.py:539
  178.3 21.3 %collective-permute-start.34 = (bf16[416,384]{1,0:T(8,128)(2,1)S(1)}, bf16[416,384]{1,0:T(8,128)(2,1)S(1)}, u32[]{:S(2)}, u32[]{:S(2)}) collective-permute-start(bf16[416,384]{1,0:T(8,128)(2,1)S(1)} %dynamic-slice_bitcast_fusion.1.refs_0_), channel_id=1, source_target_pairs={{0,48},{16,0},{32,16},{48,32},{1,49},{17,1},{33,17},{49,33},{2,50}... | collective-permute-start | bytes 958472 | tf_op jit(solution)/shard_map/ppermute | solution.py:429
  179.3 21.7 %collective-permute-start.33 = (bf16[416,384]{1,0:T(8,128)(2,1)S(1)}, bf16[416,384]{1,0:T(8,128)(2,1)S(1)}, u32[]{:S(2)}, u32[]{:S(2)}) collective-permute-start(bf16[416,384]{1,0:T(8,128)(2,1)S(1)} %dynamic-slice_bitcast_fusion.1.refs_0_), channel_id=1, source_target_pairs={{0,32},{16,48},{32,0},{48,16},{1,33},{17,49},{33,1},{49,17},{2,34}... | collective-permute-start | bytes 958472 | tf_op jit(solution)/shard_map/ppermute | solution.py:429
  180.1 22.4 %collective-permute-start.32 = (bf16[416,384]{1,0:T(8,128)(2,1)S(1)}, bf16[416,384]{1,0:T(8,128)(2,1)S(1)}, u32[]{:S(2)}, u32[]{:S(2)}) collective-permute-start(bf16[416,384]{1,0:T(8,128)(2,1)S(1)} %dynamic-slice_bitcast_fusion.1.refs_0_), channel_id=1, source_target_pairs={{0,16},{16,32},{32,48},{48,0},{1,17},{17,33},{33,49},{49,1},{2,18}... | collective-permute-start | bytes 958472 | tf_op jit(solution)/shard_map/ppermute | solution.py:429
  198.7 0.8 copy-start.12
  199.5 40.6 %copy-start.10 = (bf16[768,384]{1,0:T(8,128)(2,1)}, bf16[768,384]{1,0:T(8,128)(2,1)S(1)}, u32[]{:S(2)}) copy-start(bf16[768,384]{1,0:T(8,128)(2,1)S(1)} %get-tuple-element.305.refs_10_) | copy-start | bytes 1769476
  199.6 40.6 %copy-start.18 = (bf16[384,384]{1,0:T(8,128)(2,1)}, bf16[384,384]{1,0:T(8,128)(2,1)S(1)}, u32[]{:S(2)}) copy-start(bf16[384,384]{1,0:T(8,128)(2,1)S(1)} %get-tuple-element.303.refs_15_.refs_14_) | copy-start | bytes 884740
  199.6 44.0 %collective-permute-start.31 = (bf16[2048,128]{1,0:T(8,128)(2,1)}, bf16[2048,128]{1,0:T(8,128)(2,1)}, u32[]{:S(2)}, u32[]{:S(2)}) collective-permute-start(bf16[2048,128]{1,0:T(8,128)(2,1)} %maximum_select_fusion), channel_id=1, source_target_pairs={{8,12},{11,13},{14,14},{24,28},{27,29},{30,30},{40,44},{43,45},{46... | collective-permute-start | bytes 1572872 | tf_op jit(solution)/shard_map/ppermute | solution.py:539
  201.0 42.5 %collective-permute-start.30 = (bf16[2048,128]{1,0:T(8,128)(2,1)}, bf16[2048,128]{1,0:T(8,128)(2,1)}, u32[]{:S(2)}, u32[]{:S(2)}) collective-permute-start(bf16[2048,128]{1,0:T(8,128)(2,1)} %maximum_select_fusion), channel_id=1, source_target_pairs={{7,12},{10,13},{13,14},{23,28},{26,29},{29,30},{39,44},{42,45},{45... | collective-permute-start | bytes 1572872 | tf_op jit(solution)/shard_map/ppermute | solution.py:539
  202.5 41.0 %collective-permute-start.29 = (bf16[2048,128]{1,0:T(8,128)(2,1)}, bf16[2048,128]{1,0:T(8,128)(2,1)}, u32[]{:S(2)}, u32[]{:S(2)}) collective-permute-start(bf16[2048,128]{1,0:T(8,128)(2,1)} %maximum_select_fusion), channel_id=1, source_target_pairs={{5,11},{6,12},{9,13},{12,14},{15,15},{21,27},{22,28},{25,29},{28,3... | collective-permute-start | bytes 1572872 | tf_op jit(solution)/shard_map/ppermute | solution.py:539
  240.1 1.0 copy-start.6
  241.1 0.8 copy-start.13
  241.9 0.8 copy-start.14
  (4 other events, 3.0 us)
Sparse Core Ops, SparseCore 0:
  53.6 55.7 all-reduce.1
Sparse Core Ops, SparseCore 1:
  82.6 82.1 all-gather.2
